TPU v7x, 32 devices: a whole 2x2x4 slice. The times are simulated.
32 devices in a mesh: seq: 4 (over y, core), exp: 8 (over z, x).
Axes of the slice: x: 2, y: 2, z: 4, core: 2. Of those that a mesh axis runs over, the one named last changes fastest.
Arguments:
- layer_input: bfloat16 [8, 1024, 2048], P('exp', 'seq'), may hold values from -6 to 6
- queries: bfloat16 [8, 1024, 2048], P('exp', 'seq'), may hold values from -6 to 6
- keys_in: bfloat16 [8, 1024, 2048], P('exp', 'seq'), may hold values from -0.59765625 to 0.59765625
- values_in: bfloat16 [8, 1024, 2048], P('exp', 'seq'), may hold values from -6 to 6
- decay_rate: float32 [8, 1024, 16], P('exp', 'seq'), as said below
- attn_gain: float32 [2048], replicated, may hold values from 0.25 to 1.75
- norm_gain: float32 [2048], replicated, may hold values from 0.25 to 1.75
- expert_ids: int32 [8, 1024, 2], P('exp', 'seq'), may hold values from 0 to 7, all different within a row; in each aligned block of 256 rows (0 to 255, 256 to 511, ..., all dimensions but the last counted through in order) at most 96 rows name the same one
- gate_levels: int32 [8, 1024, 2], P('exp', 'seq'), may hold values from 1 to 256
- w_gate: bfloat16 [8, 2048, 768], P('exp'), may hold values from -0.125 to 0.125
- w_up: bfloat16 [8, 2048, 768], P('exp'), may hold values from -0.125 to 0.125
- w_down: bfloat16 [8, 768, 2048], P('exp'), may hold values from -0.21875 to 0.21875
Outputs:
- layer_out: bfloat16 [8, 1024, 2048], P('exp', 'seq')
Inputs may be any that keep to these rules, and one draw needn't show every extreme that they name: `expert_ids`: each token names 2 different experts. Among the 256 positions of one device, no expert is named by more than 96 routes, a bound that some block reaches. `decay_rate`: every entry is positive.
All inputs are finite; a program needn't handle non-finite values.
Results may differ from a plain program's by a relative error of at most 0.01.
Values may be sent and summed in bfloat16 or wider, within the bound.
A program may use at most 128 MiB of HBM per device.

v0:
```python
import jax
import jax.numpy as jnp
from jax import lax
from jax.sharding import PartitionSpec as P


def prefix(shard, axis, join, neutral):
    place = lax.axis_index(axis)
    gathered = jax.tree.map(
        lambda a, kind: lax.all_gather(a.astype(kind), axis), shard, (jnp.bfloat16, jnp.bfloat16)
    )
    state = jax.tree.map(lambda a, e: jnp.zeros_like(a) + jnp.asarray(e, a.dtype), shard, neutral)

    def one(hop, state):
        return join(
            state,
            jax.tree.map(
                lambda a, own: lax.dynamic_index_in_dim(a, hop, 0, False).astype(own.dtype),
                gathered,
                shard,
            ),
        )

    return lax.fori_loop(0, place, one, state)


def expert_rows(slot_block, gate_weight, up_weight, down_weight):
    row_width = slot_block.shape[2]
    flat_rows = slot_block.reshape(-1, row_width)
    gate_part = jnp.dot(flat_rows, gate_weight, preferred_element_type=jnp.float32)
    up_part = jnp.dot(flat_rows, up_weight, preferred_element_type=jnp.float32)
    activation = (jax.nn.silu(gate_part) * up_part).astype(jnp.bfloat16)
    result = jnp.dot(activation, down_weight, preferred_element_type=jnp.float32).astype(
        jnp.bfloat16
    )
    return result.reshape(slot_block.shape)


def per_device(
    layer_input,
    queries,
    keys_in,
    values_in,
    decay_rate,
    attn_gain,
    norm_gain,
    expert_ids,
    gate_levels,
    w_gate,
    w_up,
    w_down,
):
    block_len = layer_input.shape[1]
    row_width = layer_input.shape[2]
    head_count = decay_rate.shape[2]
    head_dim = row_width // head_count
    top_count = expert_ids.shape[2]
    query_heads = queries[0].reshape(block_len, head_count, head_dim)
    key_heads = keys_in[0].reshape(block_len, head_count, head_dim)
    value_heads = values_in[0].reshape(block_len, head_count, head_dim)
    cumulative = -jnp.cumsum(decay_rate[0], axis=0)
    block_total = cumulative[-1]
    key_weighted = (
        key_heads.astype(jnp.float32) * jnp.exp(block_total[None, :] - cumulative)[:, :, None]
    )
    contrib = jnp.einsum(
        "thd,the->hde",
        key_weighted,
        value_heads.astype(jnp.float32),
        precision=lax.Precision.HIGHEST,
    )

    def combine(earlier, later_part):
        return (
            earlier[0] + later_part[0],
            jnp.exp(later_part[0])[:, None, None] * earlier[1] + later_part[1],
        )

    logs_before, carried = prefix(
        (block_total, contrib),
        "seq",
        combine,
        (jnp.zeros_like(block_total), jnp.zeros_like(contrib)),
    )
    scores = jnp.einsum("thd,shd->hts", query_heads, key_heads, preferred_element_type=jnp.float32)
    cum_heads = cumulative.T
    log_gap = cum_heads[:, :, None] - cum_heads[:, None, :]
    causal = (jnp.arange(block_len)[:, None] >= jnp.arange(block_len)[None, :])[None]
    weights = jnp.where(causal, jnp.exp(jnp.minimum(log_gap, 0.0)), 0.0)
    attn_probs = (scores * weights).astype(jnp.bfloat16)
    intra_part = jnp.einsum(
        "hts,shd->thd", attn_probs, value_heads, preferred_element_type=jnp.float32
    )
    inter_part = jnp.exp(cumulative)[:, :, None] * jnp.einsum(
        "thd,hde->the", query_heads.astype(jnp.float32), carried, precision=lax.Precision.HIGHEST
    )
    raw_attn = intra_part + inter_part
    normed_heads = raw_attn / jnp.sqrt(
        jnp.mean(raw_attn * raw_attn, axis=-1, keepdims=True) + 1e-06
    )
    h_res = (
        layer_input[0].astype(jnp.float32) + normed_heads.reshape(block_len, row_width) * attn_gain
    )
    normed = (
        norm_gain * h_res / jnp.sqrt(jnp.mean(h_res * h_res, axis=-1, keepdims=True) + 1e-06)
    ).astype(jnp.bfloat16)
    owners = lax.axis_size("exp")
    capacity = 3 * block_len // owners
    flat_ids = expert_ids[0].reshape(-1)
    onehot = (flat_ids[:, None] == jnp.arange(owners, dtype=jnp.int32)[None, :]).astype(jnp.int32)
    slot_rank = jnp.sum(jnp.cumsum(onehot, axis=0) * onehot, axis=1) - 1
    position = flat_ids * capacity + slot_rank
    routed = jnp.repeat(normed, top_count, axis=0)
    send_rows = jnp.zeros((owners * capacity, row_width), jnp.bfloat16).at[position].set(routed)
    send_rows = send_rows.reshape(owners, capacity, row_width)
    expert_done = expert_rows(
        lax.all_to_all(send_rows, "exp", split_axis=0, concat_axis=0, tiled=True),
        w_gate[0],
        w_up[0],
        w_down[0],
    )
    returned = lax.all_to_all(expert_done, "exp", split_axis=0, concat_axis=0, tiled=True)
    picked = returned.reshape(owners * capacity, row_width)[position]
    gate_scale = gate_levels[0].reshape(-1).astype(jnp.float32) / 256.0
    moe_out = jnp.sum(
        (picked.astype(jnp.float32) * gate_scale[:, None]).reshape(block_len, top_count, row_width),
        axis=1,
    )
    return (h_res + moe_out).astype(jnp.bfloat16)[None]


def solution(mesh):
    in_specs = (
        P("exp", "seq", None),
        P("exp", "seq", None),
        P("exp", "seq", None),
        P("exp", "seq", None),
        P("exp", "seq", None),
        P(),
        P(),
        P("exp", "seq", None),
        P("exp", "seq", None),
        P("exp", None, None),
        P("exp", None, None),
        P("exp", None, None),
    )
    out_specs = P("exp", "seq", None)
    return jax.shard_map(
        per_device, mesh=mesh, in_specs=in_specs, out_specs=out_specs, check_vma=False
    )
```

profile of v0, /device:TPU:12, one launch (start us, length us, event | category | flops | bytes accessed | tf_op | source)
XLA Modules:
  0.0 268.0 jit_solution(4661689797158766452)
XLA Ops:
  6.5 0.0 copy-start
  6.5 0.0 all-gather.4.cloned.1.call-start
  6.5 0.9 copy_bitcast_fusion.1
  7.4 0.6 reduce-window.14
  8.0 0.2 slice_reduce_fusion.1
  8.2 0.1 fusion.33
  8.3 0.2 slice_reduce_fusion.2
  8.4 0.1 bitcast_exponential_fusion
  8.5 2.3 copy.71
  10.8 1.5 copy.75
  12.4 0.0 copy-start.7
  12.4 0.0 copy-start.10
  12.4 1.0 copy-done.7
  13.4 0.0 copy-done.6
  13.4 2.2 fusion.17
  15.6 0.0 all-gather.4.cloned.1.call-update
  15.6 0.2 fusion.30
  15.8 5.0 %all-gather.1 = bf16[4,1,16]{2,1,0:T(2,128)(2,1)S(1)} all-gather(bf16[1,1,16]{2,1,0:T(2,128)(2,1)S(1)} %bitcast.112), channel_id=1, replica_groups=mesh['seq'=4,'exp'=8] {'seq'}, dimensions={0}, use_global_device_ids=true | all-gather | bytes 160 | tf_op jit(solution)/shard_map/all_gather | solution.py:10
  20.8 0.0 copy-done.10
  20.8 0.1 copy.65
  21.0 0.1 eq.29
  21.1 0.1 eq.25
  21.3 2.4 copy.74
  23.7 1.1 reduce-window.16
  24.8 0.2 slice_reduce_fusion
  25.1 0.1 copy.64
  25.3 0.1 mul.109
  25.4 0.1 fusion.28
  25.5 5.0 %fusion.16 = f32[16,256,128]{1,2,0:T(8,128)} fusion(bf16[256,16,128]{0,2,1:T(8,128)(2,1)} %bitcast.105, f32[16,256]{1,0:T(8,128)S(1)} %get-tuple-element.63, pred[256,256]{1,0:T(8,128)(4,1)S(1)} %iota_compare_fusion, bf16[256,16,128]{2,1,0:T(8,128)(2,1)} %bitcast.108, bf16[256,16,128]{2,1,0:T(8,128)(2,1)} %bitcast.97), kind=kOutput, calls=%fused_computation.28 | convolution fusion | flops 542113792 | bytes 5324800 | tf_op jit(solution)/shard_map/hts,shd->thd/dot_general | solution.py:91
  30.6 8.0 %all-gather.4.cloned.1.call-done = bf16[64,128,128]{2,1,0:T(8,128)(2,1)} async-done(((bf16[16,128,128]{2,1,0:T(8,128)(2,1)}), bf16[64,128,128]{2,1,0:T(8,128)(2,1)}) %all-gather.4.cloned.1.call-update) | async-done | bytes 2097168 | tf_op jit(solution)/shard_map/all_gather | solution.py:10
  38.5 1.1 broadcast_in_dim.19
  39.6 5.0 %while.12 = (s32[]{:T(128)}, f32[16,128,128]{2,1,0:T(8,128)}, s32[]{:T(128)}, bf16[4,16]{1,0:T(4,128)(2,1)S(1)}, bf16[4,16,128,128]{3,2,1,0:T(8,128)(2,1)}, /*index=5*/s32[]{:T(128)}, s32[]{:T(128)}, s32[]{:T(128)}) while((s32[]{:T(128)}, f32[16,128,128]{2,1,0:T(8,128)}, s32[]{:T(128)}, bf16[4,16]{1,0:T(4,128)(2,1)S(1)}, ...), condition=%wide.region_3.4_spmd, body=%wide.region_2.3_spmd.sunk | while | flops 786453 | bytes 2621727 | solution.py:24
  39.6 2.5 convert_add_fusion.3
  42.1 2.5 convert_add_fusion.3
  44.6 3.6 %multiply_reduce_fusion.2 = (f32[256,16]{0,1:T(8,128)S(1)}, f32[256,16,128]{0,2,1:T(8,128)S(1)}) fusion(f32[16,128,128]{2,1,0:T(8,128)} %get-tuple-element.49, bf16[256,16,128]{2,1,0:T(8,128)(2,1)} %bitcast.98, f32[256,16]{0,1:T(8,128)S(1)} %get-tuple-element.60, f32[16,256,128]{1,2,0:T(8,128)} %fusion.16), kind=kOutput, calls=%fused_computation.22 | convolution fusion | flops 807399424 | bytes 6324224 | tf_op jit(solution)/shard_map/thd,hde->the/dot_general | solution.py:94
  48.2 1.6 broadcast_divide_fusion
  49.9 3.0 %copy.67 = f32[256,2048]{1,0:T(8,128)} copy(f32[256,2048]{0,1:T(8,128)} %bitcast.94) | data formatting | bytes 4194304 | tf_op jit(solution)/shard_map/reshape | solution.py:102
  52.8 0.0 copy-done.8
  52.8 0.0 copy-start.9
  52.9 2.4 multiply_reduce_fusion.1
  55.3 0.1 copy-done.1
  55.4 0.3 copy-done.2
  55.6 0.0 copy-done.9
  55.6 0.4 divide_convert_fusion
  56.1 2.6 broadcast_in_dim.21
  58.7 4.1 %reshape.203 = bf16[512,2048]{1,0:T(8,128)(2,1)} reshape(bf16[256,2,2048]{2,1,0:T(2,128)(2,1)} %broadcast_in_dim.21) | data formatting | bytes 4194304 | tf_op jit(solution)/shard_map/reshape | solution.py:113
  62.8 6.7 %scatter_custom_fusion = bf16[768,2048]{1,0:T(8,128)(2,1)} fusion(s32[512]{0:T(512)S(1)} %bitcast.109, bf16[512,2048]{1,0:T(8,128)(2,1)} %reshape.203, bf16[]{:T(256)} %constant.52.clone.1), kind=kCustom, calls=%fused_computation.26 | custom fusion | bytes 3146240 | tf_op jit(solution)/shard_map/scatter | solution.py:114
  69.6 75.9 %all_to_all.10 = bf16[8,96,2048]{2,1,0:T(8,128)(2,1)S(1)} all-to-all(bf16[8,96,2048]{2,1,0:T(8,128)(2,1)} %bitcast.96), channel_id=1, replica_groups=mesh['seq'=4,'exp'=8] {'exp'}, dimensions={0} | all-to-all | bytes 6291456 | tf_op jit(solution)/shard_map/all_to_all | solution.py:117
  145.5 1.7 copy-done.5
  147.2 0.0 copy-done.12
  147.2 4.0 %fusion.1 = f32[768,768]{1,0:T(8,128)} fusion(bf16[768,2048]{1,0:T(8,128)(2,1)S(1)} %bitcast.101, bf16[1,2048,768]{2,1,0:T(8,128)(2,1)S(1)} %copy-done.12), kind=kOutput, calls=%fused_computation.8 | convolution fusion | flops 2415919104 | bytes 8650752 | tf_op jit(solution)/shard_map/dot_general | solution.py:31
  151.2 0.0 copy-done
  151.2 11.0 %convolution_convert_fusion = bf16[768,2048]{1,0:T(8,128)(2,1)} fusion(bf16[1,768,2048]{2,1,0:T(8,128)(2,1)S(1)} %copy-done, f32[768,768]{1,0:T(8,128)} %fusion.1, bf16[768,2048]{1,0:T(8,128)(2,1)} %bitcast.102, bf16[1,2048,768]{2,1,0:T(8,128)(2,1)} %param.23), kind=kOutput, calls=%fused_computation.6 | convolution fusion | flops 4836950016 | bytes 14942208 | tf_op jit(solution)/shard_map/dot_general | solution.py:33
  162.2 5.7 %all-to-all-start.1 = ((bf16[8,96,2048]{2,1,0:T(8,128)(2,1)}), bf16[8,96,2048]{2,1,0:T(8,128)(2,1)}, u32[]{:S(2)}, u32[]{:S(2)}) async-start(bf16[8,96,2048]{2,1,0:T(8,128)(2,1)} %bitcast.100), calls=%async_computation.1 | async-start | bytes 6291456 | tf_op jit(solution)/shard_map/all_to_all | solution.py:122
  167.9 0.0 copy-done.11
  167.9 0.1 copy.68
  168.1 2.9 %copy.63 = f32[1,256,2048]{2,1,0:T(8,128)} copy(f32[1,256,2048]{1,2,0:T(8,128)} %bitcast.95) | data formatting | bytes 4194304 | tf_op jit(solution)/shard_map/reshape | solution.py:102
  171.0 66.6 %all-to-all-done.1 = bf16[8,96,2048]{2,1,0:T(8,128)(2,1)} async-done(((bf16[8,96,2048]{2,1,0:T(8,128)(2,1)}), bf16[8,96,2048]{2,1,0:T(8,128)(2,1)}, u32[]{:S(2)}, u32[]{:S(2)}) %all-to-all-start.1) | async-done | bytes 3145760 | tf_op jit(solution)/shard_map/all_to_all | solution.py:122
  237.6 7.5 %gather_fusion = bf16[512,2048]{1,0:T(8,128)(2,1)} fusion(bf16[768,2048]{1,0:T(8,128)(2,1)} %bitcast.21, s32[1024]{0:T(1024)S(1)} %pad_clamp_fusion), kind=kCustom, calls=%fused_computation | custom fusion | bytes 4196352 | tf_op jit(solution)/shard_map/gather | solution.py:123
  245.1 5.4 %reshape.190 = f32[256,2,2048]{2,1,0:T(2,128)} reshape(bf16[512,2048]{1,0:T(8,128)(2,1)} %gather_fusion) | data formatting | bytes 6291456 | tf_op jit(solution)/shard_map/convert_element_type | solution.py:126
  250.6 9.0 %multiply_reduce_fusion = f32[256,2048]{1,0:T(8,128)S(1)} fusion(f32[256,2,2048]{2,1,0:T(2,128)} %reshape.190, f32[256,2]{1,0:T(8,128)S(1)} %copy.68), kind=kLoop, calls=%fused_computation.4 | loop fusion | flops 1572864 | bytes 6293504 | tf_op jit(solution)/shard_map/reduce_sum | solution.py:125
  259.6 0.0 copy-done.3
  259.6 0.0 copy-done.4
  259.6 1.5 fusion.6
  (25 shorter events, 0.2 us)
Async XLA Ops:
  6.5 144.7 %copy-start = (bf16[1,768,2048]{2,1,0:T(8,128)(2,1)S(1)}, bf16[1,768,2048]{2,1,0:T(8,128)(2,1)}, u32[]{:S(2)}) copy-start(bf16[1,768,2048]{2,1,0:T(8,128)(2,1)} %param.25) | copy-start | bytes 9437188
  6.5 32.0 %all-gather.4.cloned.1.call-start = ((), (), s32[]{:S(2)}) async-start(), calls=%async_computation.2 | async-start | bytes 2621440 | tf_op jit(solution)/shard_map/all_gather | solution.py:10
  10.8 2.6 copy-start.6
  12.4 1.0 copy-start.7
  12.4 8.5 %copy-start.10 = (s32[1,256,2]{1,2,0:T(2,128)S(1)}, s32[1,256,2]{1,2,0:T(2,128)}, u32[]{:S(2)}) copy-start(s32[1,256,2]{1,2,0:T(2,128)} %param.21) | copy-start | bytes 6148
  49.9 3.0 %copy-start.8 = (f32[2048]{0:T(1024)S(1)}, f32[2048]{0:T(1024)}, u32[]{:S(2)}) copy-start(f32[2048]{0:T(1024)} %param.19) | copy-start | bytes 24580
  52.8 2.5 copy-start.1
  52.8 2.8 %copy-start.2 = (bf16[1,256,2048]{2,1,0:T(8,128)(2,1)S(1)}, bf16[1,256,2048]{2,1,0:T(8,128)(2,1)}, u32[]{:S(2)}) copy-start(bf16[1,256,2048]{2,1,0:T(8,128)(2,1)} %param.14) | copy-start | bytes 3145732
  52.8 2.8 %copy-start.9 = (f32[2048]{0:T(1024)S(1)}, f32[2048]{0:T(1024)}, u32[]{:S(2)}) copy-start(f32[2048]{0:T(1024)} %param.20) | copy-start | bytes 24580
  69.6 77.7 %copy-start.12 = (bf16[1,2048,768]{2,1,0:T(8,128)(2,1)S(1)}, bf16[1,2048,768]{2,1,0:T(8,128)(2,1)}, u32[]{:S(2)}) copy-start(bf16[1,2048,768]{2,1,0:T(8,128)(2,1)} %param.24) | copy-start | bytes 9437188
  145.5 1.7 copy-start.5
  162.2 5.7 %copy-start.11 = (s32[1,256,2]{1,2,0:T(2,128)S(1)}, s32[1,256,2]{1,2,0:T(2,128)}, u32[]{:S(2)}) copy-start(s32[1,256,2]{1,2,0:T(2,128)} %param.22) | copy-start | bytes 6148
  162.2 75.3 %all-to-all-start.1 = ((bf16[8,96,2048]{2,1,0:T(8,128)(2,1)}), bf16[8,96,2048]{2,1,0:T(8,128)(2,1)}, u32[]{:S(2)}, u32[]{:S(2)}) async-start(bf16[8,96,2048]{2,1,0:T(8,128)(2,1)} %bitcast.100), calls=%async_computation.1 | async-start | bytes 6291456 | tf_op jit(solution)/shard_map/all_to_all | solution.py:122
  250.5 9.1 %copy-start.3 = (bf16[1,256,2048]{2,1,0:T(8,128)(2,1)S(1)}, bf16[1,256,2048]{2,1,0:T(8,128)(2,1)}, u32[]{:S(2)}) copy-start(bf16[1,256,2048]{2,1,0:T(8,128)(2,1)} %param.14) | copy-start | bytes 3145732
  250.6 9.1 %copy-start.4 = (f32[1,256,2048]{2,1,0:T(8,128)S(1)}, f32[1,256,2048]{2,1,0:T(8,128)}, u32[]{:S(2)}) copy-start(f32[1,256,2048]{2,1,0:T(8,128)} %copy.63) | copy-start | bytes 6291460
Sparse Core Ops, SparseCore 0:
  15.7 22.7 all-gather.3
where the time goes:
time: 271 us; the launch traced here: 268 us
  blocking collectives  81 us (30%)
  waiting for transfers between devices  74.6 us (28%)
  local copies, waits for them, and re-layouts  45.2 us (17%)
  matrix products  25.8 us (10%)
  other arithmetic  22.2 us (8%)
  between operations  13.6 us (5%)
  starting transfers between devices  5.69 us (2%)
    all_to_all x1, blocking collectives, per_device(): lax.all_to_all(send_rows, 'exp', split_axis=0, concat_axis=0, tiled=True)  75.9 us
    all_to_all x1, waiting for transfers between devices, per_device(): lax.all_to_all(expert_done, 'exp', split_axis=0, concat_axis=0, tiled=True)  66.6 us
    dot_general x1, matrix products, expert_rows(): jnp.dot(activation, down_weight, preferred_element_type=jnp.float32)  11 us
    reduce_sum x1, other arithmetic, per_device(): jnp.sum((picked.astype(jnp.float32) * gate_scale[:, None]).reshape(block_...  9.04 us
    all_gather x1, waiting for transfers between devices, prefix(): lax.all_gather(a.astype(kind), axis)  7.96 us
    gather x1, local copies, waits for them, and re-layouts, per_device(): picked = returned.reshape(owners * capacity, row_width)[position]  7.52 us
    unnamed x30, local copies, waits for them, and re-layouts  7.2 us
    scatter x1, local copies, waits for them, and re-layouts, per_device(): jnp.zeros((owners * capacity, row_width), jnp.bfloat16).at[position]  6.71 us
  transfers between devices with their start and end apart: 2, of which 2 were waited for; matrix products, arithmetic and copies ran while one was open for 5% of the time, Pallas kernels for 0%

commit v1 on v0

v1 whole, which is shorter than its diff:
```python
import functools

import jax
import jax.numpy as jnp
from jax import lax
from jax.experimental import pallas as pl
from jax.experimental.pallas import tpu as pltpu
from jax.sharding import PartitionSpec as P

MESH = pl.DeviceIdType.MESH
F32 = jnp.float32
BF16 = jnp.bfloat16


def flip(index, mask, bits):
    result = 0
    for b in range(bits):
        p = 1 << b
        result = result + p * lax.rem(lax.div(index, p) + lax.div(mask, p), 2)
    return result


def dot(a, b, contract=((1,), (0,)), **kw):
    return lax.dot_general(a, b, (contract, ((), ())), preferred_element_type=F32, **kw)


def layer_kernel(
    dims,
    x_ref,
    q_ref,
    k_ref,
    v_ref,
    decay_ref,
    attn_gain_ref,
    norm_gain_ref,
    ids_ref,
    levels_ref,
    wg_hbm,
    wu_hbm,
    wd_hbm,
    out_ref,
    wg,
    wu,
    wd,
    cum,
    cum_rows,
    logs,
    logs_before,
    contrib,
    state_out,
    pair_in,
    state_in,
    carried,
    h_res,
    normed,
    pick,
    mix,
    send,
    recv,
    act,
    done,
    back,
    weight_sem,
    pair_sem,
    log_sem,
    state_send_sem,
    state_recv_sem,
    go_send_sem,
    go_recv_sem,
    back_send_sem,
    back_recv_sem,
):
    owners, cap, seqs, heads, top = dims
    block_len, width = x_ref.shape
    dh = width // heads
    ff = wg.shape[1]
    bits = owners.bit_length() - 1
    seq = lax.axis_index("seq")
    mine = lax.axis_index("exp")
    chip = lax.div(seq, 2)
    core = lax.rem(seq, 2)

    weight_copies = [
        pltpu.make_async_copy(hbm, vmem, weight_sem.at[i])
        for i, (hbm, vmem) in enumerate(((wg_hbm, wg), (wu_hbm, wu), (wd_hbm, wd)))
    ]
    for copy in weight_copies:
        copy.start()

    barrier = pltpu.get_barrier_semaphore()
    for step in range(1, seqs):
        pl.semaphore_signal(
            barrier, inc=1, device_id={"seq": lax.rem(seq + step, seqs)}, device_id_type=MESH
        )
    for step in range(1, owners):
        pl.semaphore_signal(
            barrier, inc=1, device_id={"exp": lax.rem(mine + step, owners)}, device_id_type=MESH
        )

    down = lax.broadcasted_iota(jnp.int32, (block_len, block_len), 0)
    across = lax.broadcasted_iota(jnp.int32, (block_len, block_len), 1)
    lower = (down >= across).astype(F32)
    upper = (down <= across).astype(F32)
    rate = -decay_ref[...]
    cum[...] = dot(lower, rate, precision=lax.Precision.HIGHEST)
    cum_rows[...] = dot(rate, upper, ((0,), (0,)), precision=lax.Precision.HIGHEST)
    logs[...] = jnp.broadcast_to(cum_rows[:, block_len - 1 : block_len], logs.shape)
    lanes = lax.broadcasted_iota(jnp.int32, (block_len, heads), 1)

    def head_cum(h):
        return jnp.sum(jnp.where(lanes == h, cum[...], 0.0), axis=1, keepdims=True)

    def head_lanes(h):
        return pl.ds(pl.multiple_of(h * dh, dh), dh)

    def contrib_head(h, _):
        c = head_cum(h)
        cols = head_lanes(h)
        weight = jnp.exp(c[block_len - 1 :, :] - c)
        weighted = (k_ref[:, cols].astype(F32) * weight).astype(BF16)
        value = dot(weighted, v_ref[:, cols], ((0,), (0,)))
        contrib[h] = value
        state_out[h] = value.astype(BF16)
        return 0

    lax.fori_loop(0, heads, contrib_head, 0)
    pl.semaphore_wait(barrier, seqs - 1 + owners - 1)

    def pair_copy(target):
        return pltpu.make_async_remote_copy(
            state_out, pair_in, pair_sem.at[0], pair_sem.at[1], {"seq": target}, MESH
        )

    def log_copy(target):
        return pltpu.make_async_remote_copy(
            logs, logs_before, log_sem.at[0], log_sem.at[1], {"seq": target}, MESH
        )

    def state_copy(step):
        return pltpu.make_async_remote_copy(
            state_out,
            state_in,
            state_send_sem.at[step - 1],
            state_recv_sem,
            {"seq": lax.rem(seq + step, seqs)},
            MESH,
        )

    @pl.when(core == 0)
    def _():
        pair_copy(seq + 1).start()
        log_copy(seq + 1).start()

    expert = lax.broadcasted_iota(jnp.int32, (block_len, owners), 1)
    named = [ids_ref[:, i : i + 1] == expert for i in range(top)]
    member = sum(n.astype(F32) for n in named)
    member_bf = member.astype(BF16)
    before = (down > across).astype(BF16)
    after = (down < across).astype(BF16)
    same = (down == across).astype(BF16)
    rank = dot(before, member_bf)
    rank_rows = dot(member_bf, after, ((0,), (0,)))
    member_rows = dot(member_bf, same, ((0,), (0,)))
    place_rows = jnp.where(member_rows > 0.5, rank_rows, -1.0)
    slot = lax.broadcasted_iota(jnp.int32, (cap, block_len), 0).astype(F32)
    for e in range(owners):
        pick[e] = jnp.where(place_rows[e : e + 1, :] == slot, 1.0, 0.0).astype(BF16)
    row = rank + expert.astype(F32) * cap
    column = lax.broadcasted_iota(jnp.int32, (block_len, owners * cap), 1).astype(F32)
    total = jnp.zeros((block_len, owners * cap), F32)
    for i in range(top):
        at = jnp.sum(jnp.where(named[i], row, 0.0), axis=1, keepdims=True)
        level = levels_ref[:, i : i + 1].astype(F32) * (1.0 / 256.0)
        total = total + jnp.where(column == at, level, 0.0)
    mix[...] = total.astype(BF16)

    def decay_row(ref, h):
        return jnp.exp(ref[pl.ds(h, 1), :])

    @pl.when(core == 1)
    def _():
        pair_copy(seq).wait_recv()
        log_copy(seq).wait_recv()

        def add_pair(h, _):
            both = decay_row(logs, h) * pair_in[h].astype(F32) + contrib[h]
            contrib[h] = both
            state_out[h] = both.astype(BF16)
            return 0

        lax.fori_loop(0, heads, add_pair, 0)

        @pl.when((chip == 0) & (seqs > 2))
        def _():
            for step in (1, 2):
                state_copy(step).start()

    def intra_head(h, _):
        c = head_cum(h)
        cols = head_lanes(h)
        scores = dot(q_ref[:, cols], k_ref[:, cols], ((1,), (1,)))
        gap = c - cum_rows[pl.ds(h, 1), :]
        weight = jnp.where(down >= across, jnp.exp(jnp.minimum(gap, 0.0)), 0.0)
        probs = (scores * weight).astype(BF16)
        h_res[:, cols] = dot(probs, v_ref[:, cols])
        return 0

    lax.fori_loop(0, heads, intra_head, 0)

    @pl.when(chip > 0)
    def _():
        state_copy(1).wait_recv()

    @pl.when((core == 1) & (chip > 0) & (chip < seqs // 2 - 1))
    def _():
        def add_state(h, _):
            decay = jnp.exp(logs[pl.ds(h, 1), :] + logs_before[pl.ds(h, 1), :])
            state_out[h] = (decay * state_in[h].astype(F32) + contrib[h]).astype(BF16)
            return 0

        lax.fori_loop(0, heads, add_state, 0)
        for step in (1, 2):
            state_copy(step).start()

    @pl.when((core == 0) & (chip == 0))
    def _():
        carried[...] = jnp.zeros_like(carried)

    @pl.when((core == 0) & (chip > 0))
    def _():
        carried[...] = state_in[...]

    @pl.when((core == 1) & (chip == 0))
    def _():
        carried[...] = pair_in[...]

    @pl.when((core == 1) & (chip > 0))
    def _():
        def join(h, _):
            carried[h] = (
                decay_row(logs_before, h) * state_in[h].astype(F32) + pair_in[h].astype(F32)
            ).astype(BF16)
            return 0

        lax.fori_loop(0, heads, join, 0)

    def inter_head(h, squares):
        c = head_cum(h)
        cols = head_lanes(h)
        raw = h_res[:, cols] + jnp.exp(c) * dot(q_ref[:, cols], carried[h])
        scale = lax.rsqrt(jnp.mean(raw * raw, axis=1, keepdims=True) + 1e-6)
        res = x_ref[:, cols].astype(F32) + raw * scale * attn_gain_ref[:, cols]
        h_res[:, cols] = res
        return squares + res * res

    squares = lax.fori_loop(0, heads, inter_head, jnp.zeros((block_len, dh), F32))
    scale = lax.rsqrt(jnp.sum(squares, axis=1, keepdims=True) * (1.0 / width) + 1e-6)

    def norm_head(h, _):
        cols = head_lanes(h)
        normed[:, cols] = (h_res[:, cols] * scale * norm_gain_ref[:, cols]).astype(BF16)
        return 0

    lax.fori_loop(0, heads, norm_head, 0)

    tile = 512

    def fill(to, e, at):
        def one(n, _):
            cols = pl.ds(pl.multiple_of(n * tile, tile), tile)
            to[at, :, cols] = dot(pick[e], normed[:, cols]).astype(BF16)
            return 0

        lax.fori_loop(0, width // tile, one, 0)

    def go_copy(peer, slot):
        return pltpu.make_async_remote_copy(
            send.at[peer],
            recv.at[slot],
            go_send_sem.at[peer],
            go_recv_sem.at[slot],
            {"exp": peer},
            MESH,
        )

    def back_copy(peer, slot):
        return pltpu.make_async_remote_copy(
            done.at[peer],
            back.at[slot],
            back_send_sem.at[peer],
            back_recv_sem.at[slot],
            {"exp": peer},
            MESH,
        )

    def dispatch(j, _):
        peer = flip(mine, owners - 1 - j, bits)
        fill(send, peer, peer)
        go_copy(peer, mine).start()
        return 0

    lax.fori_loop(0, owners - 1, dispatch, 0)
    fill(recv, mine, mine)
    for copy in weight_copies:
        copy.wait()

    def run_expert(source, to):
        def up(n, _):
            cols = pl.ds(pl.multiple_of(n * 256, 256), 256)
            gate_part = dot(recv[source], wg[:, cols])
            up_part = dot(recv[source], wu[:, cols])
            act[:, cols] = (gate_part / (1.0 + jnp.exp(-gate_part)) * up_part).astype(BF16)
            return 0

        lax.fori_loop(0, ff // 256, up, 0)

        def down_part(n, _):
            cols = pl.ds(pl.multiple_of(n * tile, tile), tile)
            to[source, :, cols] = dot(act[...], wd[:, cols]).astype(BF16)
            return 0

        lax.fori_loop(0, width // tile, down_part, 0)

    run_expert(mine, back)

    def serve(j, _):
        peer = flip(mine, owners - 1 - j, bits)
        go_copy(peer, peer).wait_recv()
        run_expert(peer, done)
        back_copy(peer, mine).start()
        return 0

    lax.fori_loop(0, owners - 1, serve, 0)

    def collect(j, _):
        peer = flip(mine, owners - 1 - j, bits)
        back_copy(peer, peer).wait_recv()
        return 0

    lax.fori_loop(0, owners - 1, collect, 0)

    def combine(n, _):
        cols = pl.ds(pl.multiple_of(n * tile, tile), tile)
        rows = back[:, :, cols].reshape(owners * cap, tile)
        out_ref[:, cols] = (h_res[:, cols] + dot(mix[...], rows)).astype(BF16)
        return 0

    lax.fori_loop(0, width // tile, combine, 0)

    def drain(j, _):
        peer = flip(mine, owners - 1 - j, bits)
        go_copy(peer, mine).wait_send()
        back_copy(peer, mine).wait_send()
        return 0

    lax.fori_loop(0, owners - 1, drain, 0)

    @pl.when(core == 0)
    def _():
        pair_copy(seq + 1).wait_send()
        log_copy(seq + 1).wait_send()

    @pl.when((core == 1) & (chip < seqs // 2 - 1))
    def _():
        for step in (1, 2):
            state_copy(step).wait_send()


def per_device(
    layer_input,
    queries,
    keys_in,
    values_in,
    decay_rate,
    attn_gain,
    norm_gain,
    expert_ids,
    gate_levels,
    w_gate,
    w_up,
    w_down,
):
    block_len, width = layer_input.shape[1:]
    heads = decay_rate.shape[2]
    dh = width // heads
    top = expert_ids.shape[2]
    ff = w_gate.shape[2]
    owners = lax.axis_size("exp")
    seqs = lax.axis_size("seq")
    cap = -(-(3 * block_len // owners) // 16) * 16
    vmem = pl.BlockSpec(memory_space=pltpu.VMEM)
    hbm = pl.BlockSpec(memory_space=pl.ANY)
    state = pltpu.VMEM((heads, dh, dh), BF16)
    rows = pltpu.VMEM((owners, cap, width), BF16)
    dma = pltpu.SemaphoreType.DMA
    out = pl.pallas_call(
        functools.partial(layer_kernel, (owners, cap, seqs, heads, top)),
        out_shape=jax.ShapeDtypeStruct((block_len, width), BF16),
        in_specs=[vmem] * 9 + [hbm] * 3,
        out_specs=vmem,
        scratch_shapes=[
            pltpu.VMEM((width, ff), BF16),
            pltpu.VMEM((width, ff), BF16),
            pltpu.VMEM((ff, width), BF16),
            pltpu.VMEM((block_len, heads), F32),
            pltpu.VMEM((heads, block_len), F32),
            pltpu.VMEM((heads, dh), F32),
            pltpu.VMEM((heads, dh), F32),
            pltpu.VMEM((heads, dh, dh), F32),
            state,
            state,
            state,
            state,
            pltpu.VMEM((block_len, width), F32),
            pltpu.VMEM((block_len, width), BF16),
            pltpu.VMEM((owners, cap, block_len), BF16),
            pltpu.VMEM((block_len, owners * cap), BF16),
            rows,
            rows,
            pltpu.VMEM((cap, ff), BF16),
            rows,
            rows,
            dma((3,)),
            dma((2,)),
            dma((2,)),
            dma((2,)),
            dma,
            dma((owners,)),
            dma((owners,)),
            dma((owners,)),
            dma((owners,)),
        ],
        compiler_params=pltpu.CompilerParams(
            collective_id=0, has_side_effects=True, vmem_limit_bytes=56 * 1024 * 1024
        ),
    )(
        layer_input[0],
        queries[0],
        keys_in[0],
        values_in[0],
        decay_rate[0],
        attn_gain[None],
        norm_gain[None],
        expert_ids[0],
        gate_levels[0],
        w_gate[0],
        w_up[0],
        w_down[0],
    )
    return out[None]


def solution(mesh):
    tokens = P("exp", "seq", None)
    experts = P("exp", None, None)
    return jax.shard_map(
        per_device,
        mesh=mesh,
        in_specs=(tokens,) * 5 + (P(), P()) + (tokens,) * 2 + (experts,) * 3,
        out_specs=tokens,
        check_vma=False,
    )
```

time: 271 us -> 176 us (0.65)
  the two profiles are of different devices: /device:TPU:12 before, /device:TPU:1 now
where the time goes in v1:
time: 176 us; the launch traced here: 175 us
  Pallas kernels  169 us (96%)
  local copies, waits for them, and re-layouts  6.71 us (4%)
    pallas_call x1, Pallas kernels, per_device(): pl.pallas_call(functools.partial(layer_kernel, (owners, cap, seqs, heads,...  169 us
    unnamed x4, local copies, waits for them, and re-layouts  6.71 us

profile of v1, /device:TPU:1, one launch (start us, length us, event | category | flops | bytes accessed | tf_op | source)
XLA Modules:
  0.0 175.4 jit_solution(16118023021929167615)
XLA Ops:
  0.0 1.5 copy.13
  1.5 1.5 copy.14
  2.9 1.5 copy.15
  4.4 168.7 %shard_map.118 = bf16[256,2048]{1,0:T(8,128)(2,1)} custom-call(bf16[256,2048]{1,0:T(8,128)(2,1)} %bitcast.17, bf16[256,2048]{1,0:T(8,128)(2,1)} %bitcast.18, bf16[256,2048]{1,0:T(8,128)(2,1)} %bitcast.19, bf16[256,2048]{1,0:T(8,128)(2,1)} %bitcast.20, f32[256,16]{1,0:T(8,128)} %bitcast.21, f32[1,2048]{1,0:T(1,128)} %bitcast.24, f32[1,2048]{1,0:T(1,128)} %bitcast.25, ...), custom_call_target="tpu_custom_call" | custom-call | tf_op jit(solution)/shard_map/pallas_call | solution.py:396
  173.1 2.3 %copy.17 = bf16[1,256,2048]{2,1,0:T(8,128)(2,1)} copy(bf16[1,256,2048]{2,1,0:T(8,128)(2,1)} %bitcast.13) | data formatting | bytes 2097152

commit v2 on v1

--- a/solution.py
+++ b/solution.py
@@ -10,6 +10,8 @@
 MESH = pl.DeviceIdType.MESH
 F32 = jnp.float32
 BF16 = jnp.bfloat16
+PARTS = 4
+UNROLL = 2
 
 
 def flip(index, mask, bits):
@@ -53,6 +55,9 @@
     carried,
     h_res,
     normed,
+    relay,
+    info,
+    info_in,
     pick,
     mix,
     send,
@@ -60,25 +65,37 @@
     act,
     done,
     back,
+    part_out,
+    part_in,
     weight_sem,
     pair_sem,
     log_sem,
     state_send_sem,
     state_recv_sem,
+    info_sem,
+    relay_send_sem,
+    relay_recv_sem,
     go_send_sem,
     go_recv_sem,
     back_send_sem,
     back_recv_sem,
+    part_send_sem,
+    part_recv_sem,
 ):
     owners, cap, seqs, heads, top = dims
     block_len, width = x_ref.shape
     dh = width // heads
     ff = wg.shape[1]
-    bits = owners.bit_length() - 1
+    half = owners // 2
+    bits = half.bit_length() - 1
+    parts, _, tile = normed.shape
     seq = lax.axis_index("seq")
     mine = lax.axis_index("exp")
     chip = lax.div(seq, 2)
     core = lax.rem(seq, 2)
+    place = lax.rem(mine, half)
+    base = mine - place
+    partner = lax.rem(mine + half, owners)
 
     weight_copies = [
         pltpu.make_async_copy(hbm, vmem, weight_sem.at[i])
@@ -92,18 +109,22 @@
         pl.semaphore_signal(
             barrier, inc=1, device_id={"seq": lax.rem(seq + step, seqs)}, device_id_type=MESH
         )
-    for step in range(1, owners):
+    for step in range(1, half):
         pl.semaphore_signal(
-            barrier, inc=1, device_id={"exp": lax.rem(mine + step, owners)}, device_id_type=MESH
-        )
+            barrier,
+            inc=1,
+            device_id={"exp": base + lax.rem(place + step, half)},
+            device_id_type=MESH,
+        )
+    pl.semaphore_signal(barrier, inc=1, device_id={"exp": partner}, device_id_type=MESH)
 
     down = lax.broadcasted_iota(jnp.int32, (block_len, block_len), 0)
     across = lax.broadcasted_iota(jnp.int32, (block_len, block_len), 1)
     lower = (down >= across).astype(F32)
     upper = (down <= across).astype(F32)
     rate = -decay_ref[...]
-    cum[...] = dot(lower, rate, precision=lax.Precision.HIGHEST)
-    cum_rows[...] = dot(rate, upper, ((0,), (0,)), precision=lax.Precision.HIGHEST)
+    cum[...] = dot(lower, rate, ((1,), (1,)), precision=lax.Precision.HIGHEST)
+    cum_rows[...] = dot(rate, upper, precision=lax.Precision.HIGHEST)
     logs[...] = jnp.broadcast_to(cum_rows[:, block_len - 1 : block_len], logs.shape)
     lanes = lax.broadcasted_iota(jnp.int32, (block_len, heads), 1)
 
@@ -123,8 +144,8 @@
         state_out[h] = value.astype(BF16)
         return 0
 
-    lax.fori_loop(0, heads, contrib_head, 0)
-    pl.semaphore_wait(barrier, seqs - 1 + owners - 1)
+    lax.fori_loop(0, heads, contrib_head, 0, unroll=UNROLL)
+    pl.semaphore_wait(barrier, seqs - 1 + half)
 
     def pair_copy(target):
         return pltpu.make_async_remote_copy(
@@ -151,28 +172,19 @@
         pair_copy(seq + 1).start()
         log_copy(seq + 1).start()
 
-    expert = lax.broadcasted_iota(jnp.int32, (block_len, owners), 1)
-    named = [ids_ref[:, i : i + 1] == expert for i in range(top)]
-    member = sum(n.astype(F32) for n in named)
-    member_bf = member.astype(BF16)
-    before = (down > across).astype(BF16)
+    expert = lax.broadcasted_iota(jnp.int32, (owners, block_len), 0)
+    named = [(ids_ref[i : i + 1, :] == expert).astype(F32) for i in range(top)]
+    member = sum(named)
     after = (down < across).astype(BF16)
-    same = (down == across).astype(BF16)
-    rank = dot(before, member_bf)
-    rank_rows = dot(member_bf, after, ((0,), (0,)))
-    member_rows = dot(member_bf, same, ((0,), (0,)))
-    place_rows = jnp.where(member_rows > 0.5, rank_rows, -1.0)
-    slot = lax.broadcasted_iota(jnp.int32, (cap, block_len), 0).astype(F32)
-    for e in range(owners):
-        pick[e] = jnp.where(place_rows[e : e + 1, :] == slot, 1.0, 0.0).astype(BF16)
-    row = rank + expert.astype(F32) * cap
-    column = lax.broadcasted_iota(jnp.int32, (block_len, owners * cap), 1).astype(F32)
-    total = jnp.zeros((block_len, owners * cap), F32)
-    for i in range(top):
-        at = jnp.sum(jnp.where(named[i], row, 0.0), axis=1, keepdims=True)
-        level = levels_ref[:, i : i + 1].astype(F32) * (1.0 / 256.0)
-        total = total + jnp.where(column == at, level, 0.0)
-    mix[...] = total.astype(BF16)
+    rank = dot(member.astype(BF16), after)
+    info[0] = jnp.where(member > 0.5, rank, -1.0)
+    info[1] = sum(
+        named[i] * (levels_ref[i : i + 1, :].astype(F32) * (1.0 / 256.0)) for i in range(top)
+    )
+    info_copy = pltpu.make_async_remote_copy(
+        info, info_in, info_sem.at[0], info_sem.at[1], {"exp": partner}, MESH
+    )
+    info_copy.start()
 
     def decay_row(ref, h):
         return jnp.exp(ref[pl.ds(h, 1), :])
@@ -205,7 +217,22 @@
         h_res[:, cols] = dot(probs, v_ref[:, cols])
         return 0
 
-    lax.fori_loop(0, heads, intra_head, 0)
+    lax.fori_loop(0, heads, intra_head, 0, unroll=UNROLL)
+
+    slot = lax.broadcasted_iota(jnp.int32, (cap, block_len), 0).astype(F32)
+    same = (down == across).astype(BF16)
+
+    def slots(group, source):
+        spread = []
+        for n in range(half):
+            hit = source[0, pl.ds(base + n, 1), :] == slot
+            pick[group, n] = jnp.where(hit, 1.0, 0.0).astype(BF16)
+            spread.append(jnp.where(hit, source[1, pl.ds(base + n, 1), :], 0.0).astype(BF16))
+        mix[group] = dot(same, jnp.concatenate(spread, axis=0), ((1,), (1,))).astype(BF16)
+
+    slots(0, info)
+    info_copy.wait_recv()
+    slots(1, info_in)
 
     @pl.when(chip > 0)
     def _():
@@ -253,107 +280,134 @@
         h_res[:, cols] = res
         return squares + res * res
 
-    squares = lax.fori_loop(0, heads, inter_head, jnp.zeros((block_len, dh), F32))
+    squares = lax.fori_loop(
+        0, heads, inter_head, jnp.zeros((block_len, dh), F32), unroll=UNROLL
+    )
     scale = lax.rsqrt(jnp.sum(squares, axis=1, keepdims=True) * (1.0 / width) + 1e-6)
 
-    def norm_head(h, _):
-        cols = head_lanes(h)
-        normed[:, cols] = (h_res[:, cols] * scale * norm_gain_ref[:, cols]).astype(BF16)
-        return 0
-
-    lax.fori_loop(0, heads, norm_head, 0)
-
-    tile = 512
-
-    def fill(to, e, at):
+    def part_cols(c):
+        return pl.ds(c * tile, tile)
+
+    def relay_copy(c):
+        return pltpu.make_async_remote_copy(
+            normed.at[c],
+            relay.at[c],
+            relay_send_sem.at[c],
+            relay_recv_sem.at[c],
+            {"exp": partner},
+            MESH,
+        )
+
+    def part_copy(c):
+        return pltpu.make_async_remote_copy(
+            part_out.at[c],
+            part_in.at[c],
+            part_send_sem.at[c],
+            part_recv_sem.at[c],
+            {"exp": partner},
+            MESH,
+        )
+
+    def near_copy(source, target, send_sem, recv_sem, group, c, peer, slot):
+        if group == 0:
+            source, target = source.at[0, peer], target.at[0, slot]
+        else:
+            source, target = source.at[1, peer, c], target.at[1, slot, c]
+        return pltpu.make_async_remote_copy(
+            source,
+            target,
+            send_sem.at[group, peer, c],
+            recv_sem.at[group, slot, c],
+            {"exp": base + peer},
+            MESH,
+        )
+
+    def go_copy(group, c, peer, slot):
+        return near_copy(send, recv, go_send_sem, go_recv_sem, group, c, peer, slot)
+
+    def back_copy(group, c, peer, slot):
+        return near_copy(done, back, back_send_sem, back_recv_sem, group, c, peer, slot)
+
+    def each_peer(action):
+        def one(j, _):
+            action(flip(place, half - 1 - j, bits))
+            return 0
+
+        lax.fori_loop(0, half - 1, one, 0)
+
+    def fill(group, c, source):
+        rows = dot(pick[group].reshape(half * cap, block_len), source[c])
+        send[group, :, c] = rows.astype(BF16).reshape(half, cap, tile)
+        recv[group, place, c] = send[group, place, c]
+
+    def run_up(group):
         def one(n, _):
-            cols = pl.ds(pl.multiple_of(n * tile, tile), tile)
-            to[at, :, cols] = dot(pick[e], normed[:, cols]).astype(BF16)
+            cols = pl.ds(pl.multiple_of(n * 256, 256), 256)
+            gate_part = up_part = 0.0
+            for c in range(parts):
+                rows = recv[group, :, c].reshape(half * cap, tile)
+                gate_part = gate_part + dot(rows, wg[part_cols(c), cols])
+                up_part = up_part + dot(rows, wu[part_cols(c), cols])
+            act[:, cols] = (gate_part / (1.0 + jnp.exp(-gate_part)) * up_part).astype(BF16)
             return 0
 
-        lax.fori_loop(0, width // tile, one, 0)
-
-    def go_copy(peer, slot):
-        return pltpu.make_async_remote_copy(
-            send.at[peer],
-            recv.at[slot],
-            go_send_sem.at[peer],
-            go_recv_sem.at[slot],
-            {"exp": peer},
-            MESH,
-        )
-
-    def back_copy(peer, slot):
-        return pltpu.make_async_remote_copy(
-            done.at[peer],
-            back.at[slot],
-            back_send_sem.at[peer],
-            back_recv_sem.at[slot],
-            {"exp": peer},
-            MESH,
-        )
-
-    def dispatch(j, _):
-        peer = flip(mine, owners - 1 - j, bits)
-        fill(send, peer, peer)
-        go_copy(peer, mine).start()
-        return 0
-
-    lax.fori_loop(0, owners - 1, dispatch, 0)
-    fill(recv, mine, mine)
+        lax.fori_loop(0, ff // 256, one, 0)
+
+    def run_down(group, c):
+        rows = dot(act[...], wd[:, part_cols(c)]).astype(BF16)
+        done[group, :, c] = rows.reshape(half, cap, tile)
+        back[group, place, c] = done[group, place, c]
+
+    for c in range(parts):
+        normed[c] = (h_res[:, part_cols(c)] * scale * norm_gain_ref[:, part_cols(c)]).astype(BF16)
+        relay_copy(c).start()
+    for c in range(parts):
+        fill(0, c, normed)
+    each_peer(lambda peer: go_copy(0, 0, peer, place).start())
     for copy in weight_copies:
         copy.wait()
 
-    def run_expert(source, to):
-        def up(n, _):
-            cols = pl.ds(pl.multiple_of(n * 256, 256), 256)
-            gate_part = dot(recv[source], wg[:, cols])
-            up_part = dot(recv[source], wu[:, cols])
-            act[:, cols] = (gate_part / (1.0 + jnp.exp(-gate_part)) * up_part).astype(BF16)
-            return 0
-
-        lax.fori_loop(0, ff // 256, up, 0)
-
-        def down_part(n, _):
-            cols = pl.ds(pl.multiple_of(n * tile, tile), tile)
-            to[source, :, cols] = dot(act[...], wd[:, cols]).astype(BF16)
-            return 0
-
-        lax.fori_loop(0, width // tile, down_part, 0)
-
-    run_expert(mine, back)
-
-    def serve(j, _):
-        peer = flip(mine, owners - 1 - j, bits)
-        go_copy(peer, peer).wait_recv()
-        run_expert(peer, done)
-        back_copy(peer, mine).start()
-        return 0
-
-    lax.fori_loop(0, owners - 1, serve, 0)
-
-    def collect(j, _):
-        peer = flip(mine, owners - 1 - j, bits)
-        back_copy(peer, peer).wait_recv()
-        return 0
-
-    lax.fori_loop(0, owners - 1, collect, 0)
-
-    def combine(n, _):
-        cols = pl.ds(pl.multiple_of(n * tile, tile), tile)
-        rows = back[:, :, cols].reshape(owners * cap, tile)
-        out_ref[:, cols] = (h_res[:, cols] + dot(mix[...], rows)).astype(BF16)
-        return 0
-
-    lax.fori_loop(0, width // tile, combine, 0)
-
-    def drain(j, _):
-        peer = flip(mine, owners - 1 - j, bits)
-        go_copy(peer, mine).wait_send()
-        back_copy(peer, mine).wait_send()
-        return 0
-
-    lax.fori_loop(0, owners - 1, drain, 0)
+    for c in range(parts):
+        if c == parts - 1:
+            each_peer(lambda peer: go_copy(0, 0, peer, peer).wait_recv())
+            run_up(0)
+            for d in range(parts):
+                run_down(0, d)
+            each_peer(lambda peer: back_copy(0, 0, peer, place).start())
+        relay_copy(c).wait_recv()
+        fill(1, c, relay)
+        each_peer(lambda peer, c=c: go_copy(1, c, peer, place).start())
+
+    for c in range(parts):
+        each_peer(lambda peer, c=c: go_copy(1, c, peer, peer).wait_recv())
+    run_up(1)
+    for c in range(parts):
+        run_down(1, c)
+        each_peer(lambda peer, c=c: back_copy(1, c, peer, place).start())
+
+    def mixed(group, c):
+        return dot(mix[group], back[group, :, c].reshape(half * cap, tile))
+
+    for c in range(parts):
+        each_peer(lambda peer, c=c: back_copy(1, c, peer, peer).wait_recv())
+        part_out[c] = mixed(1, c).astype(BF16)
+        part_copy(c).start()
+
+    each_peer(lambda peer: back_copy(0, 0, peer, peer).wait_recv())
+    for c in range(parts):
+        h_res[:, part_cols(c)] += mixed(0, c)
+    for c in range(parts):
+        part_copy(c).wait_recv()
+        out_ref[:, part_cols(c)] = (h_res[:, part_cols(c)] + part_in[c].astype(F32)).astype(BF16)
+
+    info_copy.wait_send()
+    for c in range(parts):
+        relay_copy(c).wait_send()
+        part_copy(c).wait_send()
+        each_peer(lambda peer, c=c: go_copy(1, c, peer, place).wait_send())
+        each_peer(lambda peer, c=c: back_copy(1, c, peer, place).wait_send())
+    each_peer(lambda peer: go_copy(0, 0, peer, place).wait_send())
+    each_peer(lambda peer: back_copy(0, 0, peer, place).wait_send())
 
     @pl.when(core == 0)
     def _():
@@ -387,12 +441,17 @@
     ff = w_gate.shape[2]
     owners = lax.axis_size("exp")
     seqs = lax.axis_size("seq")
+    half = owners // 2
     cap = -(-(3 * block_len // owners) // 16) * 16
+    tile = width // PARTS
     vmem = pl.BlockSpec(memory_space=pltpu.VMEM)
     hbm = pl.BlockSpec(memory_space=pl.ANY)
     state = pltpu.VMEM((heads, dh, dh), BF16)
-    rows = pltpu.VMEM((owners, cap, width), BF16)
+    rows = pltpu.VMEM((2, half, PARTS, cap, tile), BF16)
+    columns = pltpu.VMEM((PARTS, block_len, tile), BF16)
+    known = pltpu.VMEM((2, owners, block_len), F32)
     dma = pltpu.SemaphoreType.DMA
+    near = dma((2, half, PARTS))
     out = pl.pallas_call(
         functools.partial(layer_kernel, (owners, cap, seqs, heads, top)),
         out_shape=jax.ShapeDtypeStruct((block_len, width), BF16),
@@ -412,23 +471,33 @@
             state,
             state,
             pltpu.VMEM((block_len, width), F32),
-            pltpu.VMEM((block_len, width), BF16),
-            pltpu.VMEM((owners, cap, block_len), BF16),
-            pltpu.VMEM((block_len, owners * cap), BF16),
+            columns,
+            columns,
+            known,
+            known,
+            pltpu.VMEM((2, half, cap, block_len), BF16),
+            pltpu.VMEM((2, block_len, half * cap), BF16),
             rows,
             rows,
-            pltpu.VMEM((cap, ff), BF16),
+            pltpu.VMEM((half * cap, ff), BF16),
             rows,
             rows,
+            columns,
+            columns,
             dma((3,)),
             dma((2,)),
             dma((2,)),
             dma((2,)),
             dma,
-            dma((owners,)),
-            dma((owners,)),
-            dma((owners,)),
-            dma((owners,)),
+            dma((2,)),
+            dma((PARTS,)),
+            dma((PARTS,)),
+            near,
+            near,
+            near,
+            near,
+            dma((PARTS,)),
+            dma((PARTS,)),
         ],
         compiler_params=pltpu.CompilerParams(
             collective_id=0, has_side_effects=True, vmem_limit_bytes=56 * 1024 * 1024
@@ -438,11 +507,11 @@
         queries[0],
         keys_in[0],
         values_in[0],
-        decay_rate[0],
+        decay_rate[0].T,
         attn_gain[None],
         norm_gain[None],
-        expert_ids[0],
-        gate_levels[0],
+        expert_ids[0].T,
+        gate_levels[0].T,
         w_gate[0],
         w_up[0],
         w_down[0],

time: 176 us -> 155 us (0.88)
  the two profiles are of different devices: /device:TPU:1 before, /device:TPU:0 now
where the time goes in v2:
time: 155 us
  Pallas kernels  153 us (99%)
  local copies, waits for them, and re-layouts  2.3 us (1%)
    pallas_call x1, Pallas kernels, per_device(): pl.pallas_call(functools.partial(layer_kernel, (owners, cap, seqs, heads,...  153 us

profile of v2, /device:TPU:0, one launch (start us, length us, event | category | flops | bytes accessed | tf_op | source)
XLA Modules:
  0.0 154.9 jit_solution(2198268506075585166)
XLA Ops:
  0.0 152.6 %shard_map.118 = bf16[256,2048]{1,0:T(8,128)(2,1)} custom-call(bf16[256,2048]{1,0:T(8,128)(2,1)} %bitcast.23, bf16[256,2048]{1,0:T(8,128)(2,1)} %bitcast.24, bf16[256,2048]{1,0:T(8,128)(2,1)} %bitcast.25, bf16[256,2048]{1,0:T(8,128)(2,1)} %bitcast.26, f32[16,256]{1,0:T(8,128)} %bitcast.27, f32[1,2048]{1,0:T(1,128)} %bitcast.28, f32[1,2048]{1,0:T(1,128)} %bitcast.29, ...), custom_call_target="tpu_custom_call" | custom-call | tf_op jit(solution)/shard_map/pallas_call | solution.py:455
  152.6 2.3 %copy.14 = bf16[1,256,2048]{2,1,0:T(8,128)(2,1)} copy(bf16[1,256,2048]{2,1,0:T(8,128)(2,1)} %bitcast.19) | data formatting | bytes 2097152

commit v3 on v2

--- a/solution.py
+++ b/solution.py
@@ -11,7 +11,7 @@
 F32 = jnp.float32
 BF16 = jnp.bfloat16
 PARTS = 4
-UNROLL = 2
+GROUPS = 4
 
 
 def flip(index, mask, bits):
@@ -144,12 +144,22 @@
         state_out[h] = value.astype(BF16)
         return 0
 
-    lax.fori_loop(0, heads, contrib_head, 0, unroll=UNROLL)
-    pl.semaphore_wait(barrier, seqs - 1 + half)
-
-    def pair_copy(target):
+    per_group = heads // GROUPS
+
+    def group(ref, g):
+        return ref.at[pl.ds(g * per_group, per_group)]
+
+    def each_head(g, body, start=0):
+        return lax.fori_loop(g * per_group, (g + 1) * per_group, body, start, unroll=per_group)
+
+    def pair_copy(target, g):
         return pltpu.make_async_remote_copy(
-            state_out, pair_in, pair_sem.at[0], pair_sem.at[1], {"seq": target}, MESH
+            group(state_out, g),
+            group(pair_in, g),
+            pair_sem.at[0, g],
+            pair_sem.at[1, g],
+            {"seq": target},
+            MESH,
         )
 
     def log_copy(target):
@@ -157,20 +167,54 @@
             logs, logs_before, log_sem.at[0], log_sem.at[1], {"seq": target}, MESH
         )
 
-    def state_copy(step):
+    def state_copy(step, g):
         return pltpu.make_async_remote_copy(
-            state_out,
-            state_in,
-            state_send_sem.at[step - 1],
-            state_recv_sem,
+            group(state_out, g),
+            group(state_in, g),
+            state_send_sem.at[step - 1, g],
+            state_recv_sem.at[g],
             {"seq": lax.rem(seq + step, seqs)},
             MESH,
         )
 
-    @pl.when(core == 0)
-    def _():
-        pair_copy(seq + 1).start()
-        log_copy(seq + 1).start()
+    def decay_row(ref, h):
+        return jnp.exp(ref[pl.ds(h, 1), :])
+
+    def add_pair(h, _):
+        both = decay_row(logs, h) * pair_in[h].astype(F32) + contrib[h]
+        contrib[h] = both
+        state_out[h] = both.astype(BF16)
+        return 0
+
+    for g in range(GROUPS + 1):
+        if g < GROUPS:
+            each_head(g, contrib_head)
+        if g == 0:
+            pl.semaphore_wait(barrier, seqs - 1 + half)
+
+            @pl.when(core == 0)
+            def _():
+                log_copy(seq + 1).start()
+
+        if g < GROUPS:
+
+            @pl.when(core == 0)
+            def _(g=g):
+                pair_copy(seq + 1, g).start()
+
+        if g > 0:
+
+            @pl.when(core == 1)
+            def _(g=g - 1):
+                if g == 0:
+                    log_copy(seq).wait_recv()
+                pair_copy(seq, g).wait_recv()
+                each_head(g, add_pair)
+
+                @pl.when((chip == 0) & (seqs > 2))
+                def _():
+                    for step in (1, 2):
+                        state_copy(step, g).start()
 
     expert = lax.broadcasted_iota(jnp.int32, (owners, block_len), 0)
     named = [(ids_ref[i : i + 1, :] == expert).astype(F32) for i in range(top)]
@@ -186,27 +230,6 @@
     )
     info_copy.start()
 
-    def decay_row(ref, h):
-        return jnp.exp(ref[pl.ds(h, 1), :])
-
-    @pl.when(core == 1)
-    def _():
-        pair_copy(seq).wait_recv()
-        log_copy(seq).wait_recv()
-
-        def add_pair(h, _):
-            both = decay_row(logs, h) * pair_in[h].astype(F32) + contrib[h]
-            contrib[h] = both
-            state_out[h] = both.astype(BF16)
-            return 0
-
-        lax.fori_loop(0, heads, add_pair, 0)
-
-        @pl.when((chip == 0) & (seqs > 2))
-        def _():
-            for step in (1, 2):
-                state_copy(step).start()
-
     def intra_head(h, _):
         c = head_cum(h)
         cols = head_lanes(h)
@@ -217,7 +240,7 @@
         h_res[:, cols] = dot(probs, v_ref[:, cols])
         return 0
 
-    lax.fori_loop(0, heads, intra_head, 0, unroll=UNROLL)
+    lax.fori_loop(0, heads, intra_head, 0, unroll=per_group)
 
     slot = lax.broadcasted_iota(jnp.int32, (cap, block_len), 0).astype(F32)
     same = (down == across).astype(BF16)
@@ -234,42 +257,45 @@
     info_copy.wait_recv()
     slots(1, info_in)
 
-    @pl.when(chip > 0)
-    def _():
-        state_copy(1).wait_recv()
-
-    @pl.when((core == 1) & (chip > 0) & (chip < seqs // 2 - 1))
-    def _():
-        def add_state(h, _):
-            decay = jnp.exp(logs[pl.ds(h, 1), :] + logs_before[pl.ds(h, 1), :])
-            state_out[h] = (decay * state_in[h].astype(F32) + contrib[h]).astype(BF16)
-            return 0
-
-        lax.fori_loop(0, heads, add_state, 0)
-        for step in (1, 2):
-            state_copy(step).start()
-
-    @pl.when((core == 0) & (chip == 0))
-    def _():
-        carried[...] = jnp.zeros_like(carried)
-
-    @pl.when((core == 0) & (chip > 0))
-    def _():
-        carried[...] = state_in[...]
-
-    @pl.when((core == 1) & (chip == 0))
-    def _():
-        carried[...] = pair_in[...]
-
-    @pl.when((core == 1) & (chip > 0))
-    def _():
-        def join(h, _):
-            carried[h] = (
-                decay_row(logs_before, h) * state_in[h].astype(F32) + pair_in[h].astype(F32)
-            ).astype(BF16)
-            return 0
-
-        lax.fori_loop(0, heads, join, 0)
+    def add_state(h, _):
+        decay = jnp.exp(logs[pl.ds(h, 1), :] + logs_before[pl.ds(h, 1), :])
+        state_out[h] = (decay * state_in[h].astype(F32) + contrib[h]).astype(BF16)
+        return 0
+
+    def join(h, _):
+        carried[h] = (
+            decay_row(logs_before, h) * state_in[h].astype(F32) + pair_in[h].astype(F32)
+        ).astype(BF16)
+        return 0
+
+    def carry(g):
+        to, before, passed = group(carried, g), group(pair_in, g), group(state_in, g)
+
+        @pl.when(chip > 0)
+        def _():
+            state_copy(1, g).wait_recv()
+
+        @pl.when((core == 1) & (chip > 0) & (chip < seqs // 2 - 1))
+        def _():
+            each_head(g, add_state)
+            for step in (1, 2):
+                state_copy(step, g).start()
+
+        @pl.when((core == 0) & (chip == 0))
+        def _():
+            to[...] = jnp.zeros_like(to)
+
+        @pl.when((core == 0) & (chip > 0))
+        def _():
+            to[...] = passed[...]
+
+        @pl.when((core == 1) & (chip == 0))
+        def _():
+            to[...] = before[...]
+
+        @pl.when((core == 1) & (chip > 0))
+        def _():
+            each_head(g, join)
 
     def inter_head(h, squares):
         c = head_cum(h)
@@ -280,9 +306,10 @@
         h_res[:, cols] = res
         return squares + res * res
 
-    squares = lax.fori_loop(
-        0, heads, inter_head, jnp.zeros((block_len, dh), F32), unroll=UNROLL
-    )
+    squares = jnp.zeros((block_len, dh), F32)
+    for g in range(GROUPS):
+        carry(g)
+        squares = each_head(g, inter_head, squares)
     scale = lax.rsqrt(jnp.sum(squares, axis=1, keepdims=True) * (1.0 / width) + 1e-6)
 
     def part_cols(c):
@@ -348,13 +375,13 @@
                 rows = recv[group, :, c].reshape(half * cap, tile)
                 gate_part = gate_part + dot(rows, wg[part_cols(c), cols])
                 up_part = up_part + dot(rows, wu[part_cols(c), cols])
-            act[:, cols] = (gate_part / (1.0 + jnp.exp(-gate_part)) * up_part).astype(BF16)
+            act[group, :, cols] = (gate_part / (1.0 + jnp.exp(-gate_part)) * up_part).astype(BF16)
             return 0
 
         lax.fori_loop(0, ff // 256, one, 0)
 
     def run_down(group, c):
-        rows = dot(act[...], wd[:, part_cols(c)]).astype(BF16)
+        rows = dot(act[group], wd[:, part_cols(c)]).astype(BF16)
         done[group, :, c] = rows.reshape(half, cap, tile)
         back[group, place, c] = done[group, place, c]
 
@@ -371,9 +398,6 @@
         if c == parts - 1:
             each_peer(lambda peer: go_copy(0, 0, peer, peer).wait_recv())
             run_up(0)
-            for d in range(parts):
-                run_down(0, d)
-            each_peer(lambda peer: back_copy(0, 0, peer, place).start())
         relay_copy(c).wait_recv()
         fill(1, c, relay)
         each_peer(lambda peer, c=c: go_copy(1, c, peer, place).start())
@@ -384,6 +408,9 @@
     for c in range(parts):
         run_down(1, c)
         each_peer(lambda peer, c=c: back_copy(1, c, peer, place).start())
+    for c in range(parts):
+        run_down(0, c)
+    each_peer(lambda peer: back_copy(0, 0, peer, place).start())
 
     def mixed(group, c):
         return dot(mix[group], back[group, :, c].reshape(half * cap, tile))
@@ -411,13 +438,15 @@
 
     @pl.when(core == 0)
     def _():
-        pair_copy(seq + 1).wait_send()
         log_copy(seq + 1).wait_send()
+        for g in range(GROUPS):
+            pair_copy(seq + 1, g).wait_send()
 
     @pl.when((core == 1) & (chip < seqs // 2 - 1))
     def _():
-        for step in (1, 2):
-            state_copy(step).wait_send()
+        for g in range(GROUPS):
+            for step in (1, 2):
+                state_copy(step, g).wait_send()
 
 
 def per_device(
@@ -479,16 +508,16 @@
             pltpu.VMEM((2, block_len, half * cap), BF16),
             rows,
             rows,
-            pltpu.VMEM((half * cap, ff), BF16),
+            pltpu.VMEM((2, half * cap, ff), BF16),
             rows,
             rows,
             columns,
             columns,
             dma((3,)),
+            dma((2, GROUPS)),
             dma((2,)),
-            dma((2,)),
-            dma((2,)),
-            dma,
+            dma((2, GROUPS)),
+            dma((GROUPS,)),
             dma((2,)),
             dma((PARTS,)),
             dma((PARTS,)),

time: 155 us -> 146 us (0.942)
  the two profiles are of different devices: /device:TPU:0 before, /device:TPU:12 now
where the time goes in v3:
time: 146 us; the launch traced here: 145 us
  Pallas kernels  143 us (98%)
  local copies, waits for them, and re-layouts  2.3 us (2%)
    pallas_call x1, Pallas kernels, per_device(): pl.pallas_call(functools.partial(layer_kernel, (owners, cap, seqs, heads,...  143 us

profile of v3, /device:TPU:12, one launch (start us, length us, event | category | flops | bytes accessed | tf_op | source)
XLA Modules:
  0.0 145.4 jit_solution(8957783322345148658)
XLA Ops:
  0.0 143.0 %shard_map.118 = bf16[256,2048]{1,0:T(8,128)(2,1)} custom-call(bf16[256,2048]{1,0:T(8,128)(2,1)} %bitcast.23, bf16[256,2048]{1,0:T(8,128)(2,1)} %bitcast.24, bf16[256,2048]{1,0:T(8,128)(2,1)} %bitcast.25, bf16[256,2048]{1,0:T(8,128)(2,1)} %bitcast.26, f32[16,256]{1,0:T(8,128)} %bitcast.27, f32[1,2048]{1,0:T(1,128)} %bitcast.28, f32[1,2048]{1,0:T(1,128)} %bitcast.29, ...), custom_call_target="tpu_custom_call" | custom-call | tf_op jit(solution)/shard_map/pallas_call | solution.py:484
  143.1 2.3 %copy.14 = bf16[1,256,2048]{2,1,0:T(8,128)(2,1)} copy(bf16[1,256,2048]{2,1,0:T(8,128)(2,1)} %bitcast.19) | data formatting | bytes 2097152

commit v4 on v3

--- a/solution.py
+++ b/solution.py
@@ -61,10 +61,12 @@
     pick,
     mix,
     send,
+    send_on,
     recv,
     act,
     done,
     back,
+    back_on,
     part_out,
     part_in,
     weight_sem,
@@ -72,13 +74,19 @@
     log_sem,
     state_send_sem,
     state_recv_sem,
-    info_sem,
+    state_pass_sem,
+    info_send_sem,
+    info_recv_sem,
     relay_send_sem,
     relay_recv_sem,
     go_send_sem,
     go_recv_sem,
+    go_on_send_sem,
+    go_on_recv_sem,
     back_send_sem,
     back_recv_sem,
+    back_on_send_sem,
+    back_on_recv_sem,
     part_send_sem,
     part_recv_sem,
 ):
@@ -95,7 +103,18 @@
     core = lax.rem(seq, 2)
     place = lax.rem(mine, half)
     base = mine - place
-    partner = lax.rem(mine + half, owners)
+    quarter = half // 2
+    side = lax.div(mine, half)
+    line = lax.div(place, quarter)
+    low = lax.rem(place, quarter)
+    proxy = side + line == 1
+    target = (1 - side) * half + side * quarter + low
+
+    def client(i):
+        return (1 - side) * half + i * quarter + low
+
+    def proxy_place(i):
+        return (1 - side) * quarter + i
 
     weight_copies = [
         pltpu.make_async_copy(hbm, vmem, weight_sem.at[i])
@@ -116,7 +135,13 @@
             device_id={"exp": base + lax.rem(place + step, half)},
             device_id_type=MESH,
         )
-    pl.semaphore_signal(barrier, inc=1, device_id={"exp": partner}, device_id_type=MESH)
+    pl.semaphore_signal(barrier, inc=1, device_id={"exp": target}, device_id_type=MESH)
+
+    @pl.when(proxy)
+    def _():
+        for i in range(2):
+            pl.semaphore_signal(barrier, inc=1, device_id={"exp": client(i)}, device_id_type=MESH)
+
 
     down = lax.broadcasted_iota(jnp.int32, (block_len, block_len), 0)
     across = lax.broadcasted_iota(jnp.int32, (block_len, block_len), 1)
@@ -167,13 +192,23 @@
             logs, logs_before, log_sem.at[0], log_sem.at[1], {"seq": target}, MESH
         )
 
-    def state_copy(step, g):
+    def state_copy(g):
         return pltpu.make_async_remote_copy(
             group(state_out, g),
             group(state_in, g),
-            state_send_sem.at[step - 1, g],
+            state_send_sem.at[g],
             state_recv_sem.at[g],
-            {"seq": lax.rem(seq + step, seqs)},
+            {"seq": lax.rem(seq + 1 + g % 2, seqs)},
+            MESH,
+        )
+
+    def pass_copy(g):
+        return pltpu.make_async_remote_copy(
+            group(state_in, g),
+            group(state_in, g),
+            state_pass_sem.at[g],
+            state_recv_sem.at[g],
+            {"seq": seq + 1 - 2 * core},
             MESH,
         )
 
@@ -190,7 +225,14 @@
         if g < GROUPS:
             each_head(g, contrib_head)
         if g == 0:
-            pl.semaphore_wait(barrier, seqs - 1 + half)
+
+            @pl.when(proxy)
+            def _():
+                pl.semaphore_wait(barrier, seqs - 1 + half + 2)
+
+            @pl.when(jnp.logical_not(proxy))
+            def _():
+                pl.semaphore_wait(barrier, seqs - 1 + half)
 
             @pl.when(core == 0)
             def _():
@@ -213,8 +255,7 @@
 
                 @pl.when((chip == 0) & (seqs > 2))
                 def _():
-                    for step in (1, 2):
-                        state_copy(step, g).start()
+                    state_copy(g).start()
 
     expert = lax.broadcasted_iota(jnp.int32, (owners, block_len), 0)
     named = [(ids_ref[i : i + 1, :] == expert).astype(F32) for i in range(top)]
@@ -226,7 +267,7 @@
         named[i] * (levels_ref[i : i + 1, :].astype(F32) * (1.0 / 256.0)) for i in range(top)
     )
     info_copy = pltpu.make_async_remote_copy(
-        info, info_in, info_sem.at[0], info_sem.at[1], {"exp": partner}, MESH
+        info, info_in.at[line], info_send_sem, info_recv_sem.at[line], {"exp": target}, MESH
     )
     info_copy.start()
 
@@ -245,17 +286,23 @@
     slot = lax.broadcasted_iota(jnp.int32, (cap, block_len), 0).astype(F32)
     same = (down == across).astype(BF16)
 
-    def slots(group, source):
+    def slots(at, source):
         spread = []
         for n in range(half):
             hit = source[0, pl.ds(base + n, 1), :] == slot
-            pick[group, n] = jnp.where(hit, 1.0, 0.0).astype(BF16)
+            pick[at, n] = jnp.where(hit, 1.0, 0.0).astype(BF16)
             spread.append(jnp.where(hit, source[1, pl.ds(base + n, 1), :], 0.0).astype(BF16))
-        mix[group] = dot(same, jnp.concatenate(spread, axis=0), ((1,), (1,))).astype(BF16)
+        mix[at] = dot(same, jnp.concatenate(spread, axis=0), ((1,), (1,))).astype(BF16)
 
     slots(0, info)
-    info_copy.wait_recv()
-    slots(1, info_in)
+
+    @pl.when(proxy)
+    def _():
+        for i in range(2):
+            pltpu.make_async_remote_copy(
+                info, info_in.at[i], info_send_sem, info_recv_sem.at[i], {"exp": target}, MESH
+            ).wait_recv()
+            slots(1 + i, info_in.at[i])
 
     def add_state(h, _):
         decay = jnp.exp(logs[pl.ds(h, 1), :] + logs_before[pl.ds(h, 1), :])
@@ -271,15 +318,14 @@
     def carry(g):
         to, before, passed = group(carried, g), group(pair_in, g), group(state_in, g)
 
-        @pl.when(chip > 0)
+        @pl.when((chip > 0) & (core != g % 2))
         def _():
-            state_copy(1, g).wait_recv()
+            state_copy(g).wait_recv()
 
         @pl.when((core == 1) & (chip > 0) & (chip < seqs // 2 - 1))
         def _():
             each_head(g, add_state)
-            for step in (1, 2):
-                state_copy(step, g).start()
+            state_copy(g).start()
 
         @pl.when((core == 0) & (chip == 0))
         def _():
@@ -306,6 +352,13 @@
         h_res[:, cols] = res
         return squares + res * res
 
+    for g in range(GROUPS):
+
+        @pl.when((chip > 0) & (core == g % 2))
+        def _(g=g):
+            state_copy(g).wait_recv()
+            pass_copy(g).start()
+
     squares = jnp.zeros((block_len, dh), F32)
     for g in range(GROUPS):
         carry(g)
@@ -315,45 +368,65 @@
     def part_cols(c):
         return pl.ds(c * tile, tile)
 
-    def relay_copy(c):
+    def relay_copy(c, i):
         return pltpu.make_async_remote_copy(
             normed.at[c],
-            relay.at[c],
+            relay.at[i, c],
             relay_send_sem.at[c],
-            relay_recv_sem.at[c],
-            {"exp": partner},
-            MESH,
-        )
-
-    def part_copy(c):
-        return pltpu.make_async_remote_copy(
-            part_out.at[c],
+            relay_recv_sem.at[i, c],
+            {"exp": target},
+            MESH,
+        )
+
+    def part_copy(c, i):
+        return pltpu.make_async_remote_copy(
+            part_out.at[i, c],
             part_in.at[c],
-            part_send_sem.at[c],
+            part_send_sem.at[i, c],
             part_recv_sem.at[c],
-            {"exp": partner},
-            MESH,
-        )
-
-    def near_copy(source, target, send_sem, recv_sem, group, c, peer, slot):
-        if group == 0:
-            source, target = source.at[0, peer], target.at[0, slot]
-        else:
-            source, target = source.at[1, peer, c], target.at[1, slot, c]
-        return pltpu.make_async_remote_copy(
-            source,
-            target,
-            send_sem.at[group, peer, c],
-            recv_sem.at[group, slot, c],
+            {"exp": client(i)},
+            MESH,
+        )
+
+    def go_copy(peer, slot):
+        return pltpu.make_async_remote_copy(
+            send.at[peer],
+            recv.at[0, slot],
+            go_send_sem.at[peer],
+            go_recv_sem.at[slot],
             {"exp": base + peer},
             MESH,
         )
 
-    def go_copy(group, c, peer, slot):
-        return near_copy(send, recv, go_send_sem, go_recv_sem, group, c, peer, slot)
-
-    def back_copy(group, c, peer, slot):
-        return near_copy(done, back, back_send_sem, back_recv_sem, group, c, peer, slot)
+    def back_copy(peer, slot):
+        return pltpu.make_async_remote_copy(
+            done.at[0, peer],
+            back.at[slot],
+            back_send_sem.at[peer],
+            back_recv_sem.at[slot],
+            {"exp": base + peer},
+            MESH,
+        )
+
+    def go_on_copy(c, i, peer, slot):
+        return pltpu.make_async_remote_copy(
+            send_on.at[i, peer, c],
+            recv.at[1, slot, c],
+            go_on_send_sem.at[i, peer, c],
+            go_on_recv_sem.at[slot, c],
+            {"exp": base + peer},
+            MESH,
+        )
+
+    def back_on_copy(c, i, slot, at, peer):
+        return pltpu.make_async_remote_copy(
+            done.at[1, slot, c],
+            back_on.at[i, at, c],
+            back_on_send_sem.at[slot, c],
+            back_on_recv_sem.at[i, at, c],
+            {"exp": base + peer},
+            MESH,
+        )
 
     def each_peer(action):
         def one(j, _):
@@ -362,79 +435,113 @@
 
         lax.fori_loop(0, half - 1, one, 0)
 
-    def fill(group, c, source):
-        rows = dot(pick[group].reshape(half * cap, block_len), source[c])
-        send[group, :, c] = rows.astype(BF16).reshape(half, cap, tile)
-        recv[group, place, c] = send[group, place, c]
-
-    def run_up(group):
+    def each_slot(action, here=None):
+        def one(n, _):
+            at, i = proxy_place(lax.div(n, 2)), lax.rem(n, 2)
+
+            @pl.when(at != place)
+            def _():
+                action(n, at, i)
+
+            if here is not None:
+
+                @pl.when(at == place)
+                def _():
+                    here(n, i)
+
+            return 0
+
+        lax.fori_loop(0, half, one, 0)
+
+    def picked(at, source):
+        rows = dot(pick[at].reshape(half * cap, block_len), source[...])
+        return rows.astype(BF16).reshape(half, cap, tile)
+
+    def run_up(at):
         def one(n, _):
             cols = pl.ds(pl.multiple_of(n * 256, 256), 256)
             gate_part = up_part = 0.0
             for c in range(parts):
-                rows = recv[group, :, c].reshape(half * cap, tile)
+                rows = recv[at, :, c].reshape(half * cap, tile)
                 gate_part = gate_part + dot(rows, wg[part_cols(c), cols])
                 up_part = up_part + dot(rows, wu[part_cols(c), cols])
-            act[group, :, cols] = (gate_part / (1.0 + jnp.exp(-gate_part)) * up_part).astype(BF16)
+            act[at, :, cols] = (gate_part / (1.0 + jnp.exp(-gate_part)) * up_part).astype(BF16)
             return 0
 
         lax.fori_loop(0, ff // 256, one, 0)
 
-    def run_down(group, c):
-        rows = dot(act[group], wd[:, part_cols(c)]).astype(BF16)
-        done[group, :, c] = rows.reshape(half, cap, tile)
-        back[group, place, c] = done[group, place, c]
+    def run_down(at, c):
+        rows = dot(act[at], wd[:, part_cols(c)]).astype(BF16)
+        done[at, :, c] = rows.reshape(half, cap, tile)
 
     for c in range(parts):
         normed[c] = (h_res[:, part_cols(c)] * scale * norm_gain_ref[:, part_cols(c)]).astype(BF16)
-        relay_copy(c).start()
-    for c in range(parts):
-        fill(0, c, normed)
-    each_peer(lambda peer: go_copy(0, 0, peer, place).start())
+        relay_copy(c, line).start()
+    for c in range(parts):
+        send[:, c] = picked(0, normed.at[c])
+        recv[0, place, c] = send[place, c]
+    each_peer(lambda peer: go_copy(peer, place).start())
     for copy in weight_copies:
         copy.wait()
 
     for c in range(parts):
         if c == parts - 1:
-            each_peer(lambda peer: go_copy(0, 0, peer, peer).wait_recv())
+            each_peer(lambda peer: go_copy(peer, peer).wait_recv())
             run_up(0)
-        relay_copy(c).wait_recv()
-        fill(1, c, relay)
-        each_peer(lambda peer, c=c: go_copy(1, c, peer, place).start())
-
-    for c in range(parts):
-        each_peer(lambda peer, c=c: go_copy(1, c, peer, peer).wait_recv())
+
+        @pl.when(proxy)
+        def _(c=c):
+            for i in range(2):
+                slot_here = low * 2 + i
+                relay_copy(c, i).wait_recv()
+                send_on[i, :, c] = picked(1 + i, relay.at[i, c])
+                recv[1, slot_here, c] = send_on[i, place, c]
+                each_peer(lambda peer: go_on_copy(c, i, peer, slot_here).start())
+
+    for c in range(parts):
+        each_slot(lambda n, at, i, c=c: go_on_copy(c, i, at, n).wait_recv())
     run_up(1)
     for c in range(parts):
         run_down(1, c)
-        each_peer(lambda peer, c=c: back_copy(1, c, peer, place).start())
+
+        def keep(n, i, c=c):
+            back_on[i, place, c] = done[1, n, c]
+
+        each_slot(lambda n, at, i, c=c: back_on_copy(c, i, n, place, at).start(), keep)
     for c in range(parts):
         run_down(0, c)
-    each_peer(lambda peer: back_copy(0, 0, peer, place).start())
-
-    def mixed(group, c):
-        return dot(mix[group], back[group, :, c].reshape(half * cap, tile))
-
-    for c in range(parts):
-        each_peer(lambda peer, c=c: back_copy(1, c, peer, peer).wait_recv())
-        part_out[c] = mixed(1, c).astype(BF16)
-        part_copy(c).start()
-
-    each_peer(lambda peer: back_copy(0, 0, peer, peer).wait_recv())
-    for c in range(parts):
-        h_res[:, part_cols(c)] += mixed(0, c)
-    for c in range(parts):
-        part_copy(c).wait_recv()
+        back[place, c] = done[0, place, c]
+    each_peer(lambda peer: back_copy(peer, place).start())
+
+    @pl.when(proxy)
+    def _():
+        for c in range(parts):
+            for i in range(2):
+                each_peer(lambda peer: back_on_copy(c, i, peer, peer, peer).wait_recv())
+                rows = back_on[i, :, c].reshape(half * cap, tile)
+                part_out[i, c] = dot(mix[1 + i], rows).astype(BF16)
+                part_copy(c, i).start()
+
+    each_peer(lambda peer: back_copy(peer, peer).wait_recv())
+    for c in range(parts):
+        h_res[:, part_cols(c)] += dot(mix[0], back[:, c].reshape(half * cap, tile))
+    for c in range(parts):
+        part_copy(c, 0).wait_recv()
         out_ref[:, part_cols(c)] = (h_res[:, part_cols(c)] + part_in[c].astype(F32)).astype(BF16)
 
     info_copy.wait_send()
-    for c in range(parts):
-        relay_copy(c).wait_send()
-        part_copy(c).wait_send()
-        each_peer(lambda peer, c=c: go_copy(1, c, peer, place).wait_send())
-        each_peer(lambda peer, c=c: back_copy(1, c, peer, place).wait_send())
-    each_peer(lambda peer: go_copy(0, 0, peer, place).wait_send())
-    each_peer(lambda peer: back_copy(0, 0, peer, place).wait_send())
+    each_peer(lambda peer: go_copy(peer, place).wait_send())
+    each_peer(lambda peer: back_copy(peer, place).wait_send())
+    for c in range(parts):
+        relay_copy(c, line).wait_send()
+        each_slot(lambda n, at, i, c=c: back_on_copy(c, i, n, place, at).wait_send())
+
+    @pl.when(proxy)
+    def _():
+        for c in range(parts):
+            for i in range(2):
+                part_copy(c, i).wait_send()
+                each_peer(lambda peer: go_on_copy(c, i, peer, 0).wait_send())
 
     @pl.when(core == 0)
     def _():
@@ -445,8 +552,13 @@
     @pl.when((core == 1) & (chip < seqs // 2 - 1))
     def _():
         for g in range(GROUPS):
-            for step in (1, 2):
-                state_copy(step, g).wait_send()
+            state_copy(g).wait_send()
+
+    for g in range(GROUPS):
+
+        @pl.when((chip > 0) & (core == g % 2))
+        def _(g=g):
+            pass_copy(g).wait_send()
 
 
 def per_device(
@@ -476,11 +588,12 @@
     vmem = pl.BlockSpec(memory_space=pltpu.VMEM)
     hbm = pl.BlockSpec(memory_space=pl.ANY)
     state = pltpu.VMEM((heads, dh, dh), BF16)
-    rows = pltpu.VMEM((2, half, PARTS, cap, tile), BF16)
+    rows = pltpu.VMEM((half, PARTS, cap, tile), BF16)
+    two_rows = pltpu.VMEM((2, half, PARTS, cap, tile), BF16)
     columns = pltpu.VMEM((PARTS, block_len, tile), BF16)
+    two_columns = pltpu.VMEM((2, PARTS, block_len, tile), BF16)
     known = pltpu.VMEM((2, owners, block_len), F32)
     dma = pltpu.SemaphoreType.DMA
-    near = dma((2, half, PARTS))
     out = pl.pallas_call(
         functools.partial(layer_kernel, (owners, cap, seqs, heads, top)),
         out_shape=jax.ShapeDtypeStruct((block_len, width), BF16),
@@ -501,31 +614,39 @@
             state,
             pltpu.VMEM((block_len, width), F32),
             columns,
-            columns,
+            two_columns,
             known,
-            known,
-            pltpu.VMEM((2, half, cap, block_len), BF16),
-            pltpu.VMEM((2, block_len, half * cap), BF16),
+            pltpu.VMEM((2, 2, owners, block_len), F32),
+            pltpu.VMEM((3, half, cap, block_len), BF16),
+            pltpu.VMEM((3, block_len, half * cap), BF16),
             rows,
+            two_rows,
+            two_rows,
+            pltpu.VMEM((2, half * cap, ff), BF16),
+            two_rows,
             rows,
-            pltpu.VMEM((2, half * cap, ff), BF16),
-            rows,
-            rows,
-            columns,
+            two_rows,
+            two_columns,
             columns,
             dma((3,)),
             dma((2, GROUPS)),
             dma((2,)),
-            dma((2, GROUPS)),
             dma((GROUPS,)),
+            dma((GROUPS,)),
+            dma((GROUPS,)),
+            dma,
             dma((2,)),
             dma((PARTS,)),
-            dma((PARTS,)),
-            near,
-            near,
-            near,
-            near,
-            dma((PARTS,)),
+            dma((2, PARTS)),
+            dma((half,)),
+            dma((half,)),
+            dma((2, half, PARTS)),
+            dma((half, PARTS)),
+            dma((half,)),
+            dma((half,)),
+            dma((half, PARTS)),
+            dma((2, half, PARTS)),
+            dma((2, PARTS)),
             dma((PARTS,)),
         ],
         compiler_params=pltpu.CompilerParams(

time: 146 us -> 144 us (0.986)
  Pallas kernels: 143 us -> 141 us
    pallas_call x1, Pallas kernels: 143 us -> 141 us  [per_device(): pl.pallas_call(functools.partial(layer_kernel, (owners, cap, seqs, heads,...]
where the time goes in v4:
time: 144 us; the launch traced here: 143 us
  Pallas kernels  141 us (98%)
  local copies, waits for them, and re-layouts  2.3 us (2%)
    pallas_call x1, Pallas kernels, per_device(): pl.pallas_call(functools.partial(layer_kernel, (owners, cap, seqs, heads,...  141 us

profile of v4, /device:TPU:12, one launch (start us, length us, event | category | flops | bytes accessed | tf_op | source)
XLA Modules:
  0.0 143.4 jit_solution(15306185985985526610)
XLA Ops:
  0.0 141.1 %shard_map.118 = bf16[256,2048]{1,0:T(8,128)(2,1)} custom-call(bf16[256,2048]{1,0:T(8,128)(2,1)} %bitcast.23, bf16[256,2048]{1,0:T(8,128)(2,1)} %bitcast.24, bf16[256,2048]{1,0:T(8,128)(2,1)} %bitcast.25, bf16[256,2048]{1,0:T(8,128)(2,1)} %bitcast.26, f32[16,256]{1,0:T(8,128)} %bitcast.27, f32[1,2048]{1,0:T(1,128)} %bitcast.28, f32[1,2048]{1,0:T(1,128)} %bitcast.29, ...), custom_call_target="tpu_custom_call" | custom-call | tf_op jit(solution)/shard_map/pallas_call | solution.py:597
  141.1 2.3 %copy.14 = bf16[1,256,2048]{2,1,0:T(8,128)(2,1)} copy(bf16[1,256,2048]{2,1,0:T(8,128)(2,1)} %bitcast.19) | data formatting | bytes 2097152

commit v5 on v4

--- a/solution.py
+++ b/solution.py
@@ -10,7 +10,8 @@
 MESH = pl.DeviceIdType.MESH
 F32 = jnp.float32
 BF16 = jnp.bfloat16
-PARTS = 4
+PARTS = 8
+LAG = 2
 GROUPS = 4
 
 
@@ -64,6 +65,8 @@
     send_on,
     recv,
     act,
+    gate_sum,
+    up_sum,
     done,
     back,
     back_on,
@@ -457,18 +460,44 @@
         rows = dot(pick[at].reshape(half * cap, block_len), source[...])
         return rows.astype(BF16).reshape(half, cap, tile)
 
-    def run_up(at):
+    def activate(gate_part, up_part):
+        return (gate_part / (1.0 + jnp.exp(-gate_part)) * up_part).astype(BF16)
+
+    def each_hidden(action):
         def one(n, _):
-            cols = pl.ds(pl.multiple_of(n * 256, 256), 256)
+            action(pl.ds(pl.multiple_of(n * 256, 256), 256))
+            return 0
+
+        lax.fori_loop(0, ff // 256, one, 0)
+
+    def run_up():
+        def one(cols):
             gate_part = up_part = 0.0
             for c in range(parts):
-                rows = recv[at, :, c].reshape(half * cap, tile)
+                rows = recv[0, :, c].reshape(half * cap, tile)
                 gate_part = gate_part + dot(rows, wg[part_cols(c), cols])
                 up_part = up_part + dot(rows, wu[part_cols(c), cols])
-            act[at, :, cols] = (gate_part / (1.0 + jnp.exp(-gate_part)) * up_part).astype(BF16)
-            return 0
-
-        lax.fori_loop(0, ff // 256, one, 0)
+            act[0, :, cols] = activate(gate_part, up_part)
+
+        each_hidden(one)
+
+    def add_up(c):
+        each_slot(lambda n, at, i: go_on_copy(c, i, at, n).wait_recv())
+
+        def one(cols):
+            rows = recv[1, :, c].reshape(half * cap, tile)
+            gate_part = dot(rows, wg[part_cols(c), cols])
+            up_part = dot(rows, wu[part_cols(c), cols])
+            if c > 0:
+                gate_part = gate_part + gate_sum[:, cols]
+                up_part = up_part + up_sum[:, cols]
+            if c < parts - 1:
+                gate_sum[:, cols] = gate_part
+                up_sum[:, cols] = up_part
+            else:
+                act[1, :, cols] = activate(gate_part, up_part)
+
+        each_hidden(one)
 
     def run_down(at, c):
         rows = dot(act[at], wd[:, part_cols(c)]).astype(BF16)
@@ -485,10 +514,6 @@
         copy.wait()
 
     for c in range(parts):
-        if c == parts - 1:
-            each_peer(lambda peer: go_copy(peer, peer).wait_recv())
-            run_up(0)
-
         @pl.when(proxy)
         def _(c=c):
             for i in range(2):
@@ -498,9 +523,13 @@
                 recv[1, slot_here, c] = send_on[i, place, c]
                 each_peer(lambda peer: go_on_copy(c, i, peer, slot_here).start())
 
-    for c in range(parts):
-        each_slot(lambda n, at, i, c=c: go_on_copy(c, i, at, n).wait_recv())
-    run_up(1)
+        if c >= LAG:
+            add_up(c - LAG)
+
+    each_peer(lambda peer: go_copy(peer, peer).wait_recv())
+    run_up()
+    for c in range(parts - LAG, parts):
+        add_up(c)
     for c in range(parts):
         run_down(1, c)
 
@@ -623,6 +652,8 @@
             two_rows,
             two_rows,
             pltpu.VMEM((2, half * cap, ff), BF16),
+            pltpu.VMEM((half * cap, ff), F32),
+            pltpu.VMEM((half * cap, ff), F32),
             two_rows,
             rows,
             two_rows,

time: 144 us -> 140 us (0.972)
  Pallas kernels: 141 us -> 138 us
    pallas_call x1, Pallas kernels: 141 us -> 138 us  [per_device(): pl.pallas_call(functools.partial(layer_kernel, (owners, cap, seqs, heads,...]
where the time goes in v5:
time: 140 us
  Pallas kernels  138 us (99%)
  local copies, waits for them, and re-layouts  2.3 us (2%)
    pallas_call x1, Pallas kernels, per_device(): pl.pallas_call(functools.partial(layer_kernel, (owners, cap, seqs, heads,...  138 us

profile of v5, /device:TPU:12, one launch (start us, length us, event | category | flops | bytes accessed | tf_op | source)
XLA Modules:
  0.0 140.2 jit_solution(3372640733030531195)
XLA Ops:
  0.0 137.9 %shard_map.118 = bf16[256,2048]{1,0:T(8,128)(2,1)} custom-call(bf16[256,2048]{1,0:T(8,128)(2,1)} %bitcast.23, bf16[256,2048]{1,0:T(8,128)(2,1)} %bitcast.24, bf16[256,2048]{1,0:T(8,128)(2,1)} %bitcast.25, bf16[256,2048]{1,0:T(8,128)(2,1)} %bitcast.26, f32[16,256]{1,0:T(8,128)} %bitcast.27, f32[1,2048]{1,0:T(1,128)} %bitcast.28, f32[1,2048]{1,0:T(1,128)} %bitcast.29, ...), custom_call_target="tpu_custom_call" | custom-call | tf_op jit(solution)/shard_map/pallas_call | solution.py:626
  137.9 2.3 %copy.14 = bf16[1,256,2048]{2,1,0:T(8,128)(2,1)} copy(bf16[1,256,2048]{2,1,0:T(8,128)(2,1)} %bitcast.19) | data formatting | bytes 2097152

commit v6 on v5

--- a/solution.py
+++ b/solution.py
@@ -297,16 +297,6 @@
             spread.append(jnp.where(hit, source[1, pl.ds(base + n, 1), :], 0.0).astype(BF16))
         mix[at] = dot(same, jnp.concatenate(spread, axis=0), ((1,), (1,))).astype(BF16)
 
-    slots(0, info)
-
-    @pl.when(proxy)
-    def _():
-        for i in range(2):
-            pltpu.make_async_remote_copy(
-                info, info_in.at[i], info_send_sem, info_recv_sem.at[i], {"exp": target}, MESH
-            ).wait_recv()
-            slots(1 + i, info_in.at[i])
-
     def add_state(h, _):
         decay = jnp.exp(logs[pl.ds(h, 1), :] + logs_before[pl.ds(h, 1), :])
         state_out[h] = (decay * state_in[h].astype(F32) + contrib[h]).astype(BF16)
@@ -506,10 +496,19 @@
     for c in range(parts):
         normed[c] = (h_res[:, part_cols(c)] * scale * norm_gain_ref[:, part_cols(c)]).astype(BF16)
         relay_copy(c, line).start()
+    slots(0, info)
     for c in range(parts):
         send[:, c] = picked(0, normed.at[c])
         recv[0, place, c] = send[place, c]
     each_peer(lambda peer: go_copy(peer, place).start())
+    @pl.when(proxy)
+    def _():
+        for i in range(2):
+            pltpu.make_async_remote_copy(
+                info, info_in.at[i], info_send_sem, info_recv_sem.at[i], {"exp": target}, MESH
+            ).wait_recv()
+            slots(1 + i, info_in.at[i])
+
     for copy in weight_copies:
         copy.wait()
 
@@ -526,8 +525,6 @@
         if c >= LAG:
             add_up(c - LAG)
 
-    each_peer(lambda peer: go_copy(peer, peer).wait_recv())
-    run_up()
     for c in range(parts - LAG, parts):
         add_up(c)
     for c in range(parts):
@@ -537,14 +534,24 @@
             back_on[i, place, c] = done[1, n, c]
 
         each_slot(lambda n, at, i, c=c: back_on_copy(c, i, n, place, at).start(), keep)
-    for c in range(parts):
-        run_down(0, c)
-        back[place, c] = done[0, place, c]
-    each_peer(lambda peer: back_copy(peer, place).start())
+
+    def serve_own():
+        each_peer(lambda peer: go_copy(peer, peer).wait_recv())
+        run_up()
+        for c in range(parts):
+            run_down(0, c)
+            back[place, c] = done[0, place, c]
+        each_peer(lambda peer: back_copy(peer, place).start())
+
+    @pl.when(jnp.logical_not(proxy))
+    def _():
+        serve_own()
 
     @pl.when(proxy)
     def _():
         for c in range(parts):
+            if c == 2:
+                serve_own()
             for i in range(2):
                 each_peer(lambda peer: back_on_copy(c, i, peer, peer, peer).wait_recv())
                 rows = back_on[i, :, c].reshape(half * cap, tile)

time: 140 us -> 140 us (level)
  no operation moved by 1% of the time
where the time goes in v6:
time: 140 us
  Pallas kernels  138 us (99%)
  local copies, waits for them, and re-layouts  2.3 us (2%)
    pallas_call x1, Pallas kernels, per_device(): pl.pallas_call(functools.partial(layer_kernel, (owners, cap, seqs, heads,...  138 us

profile of v6, /device:TPU:12, one launch (start us, length us, event | category | flops | bytes accessed | tf_op | source)
XLA Modules:
  0.0 140.0 jit_solution(1508009491439735859)
XLA Ops:
  0.0 137.6 %shard_map.118 = bf16[256,2048]{1,0:T(8,128)(2,1)} custom-call(bf16[256,2048]{1,0:T(8,128)(2,1)} %bitcast.23, bf16[256,2048]{1,0:T(8,128)(2,1)} %bitcast.24, bf16[256,2048]{1,0:T(8,128)(2,1)} %bitcast.25, bf16[256,2048]{1,0:T(8,128)(2,1)} %bitcast.26, f32[16,256]{1,0:T(8,128)} %bitcast.27, f32[1,2048]{1,0:T(1,128)} %bitcast.28, f32[1,2048]{1,0:T(1,128)} %bitcast.29, ...), custom_call_target="tpu_custom_call" | custom-call | tf_op jit(solution)/shard_map/pallas_call | solution.py:633
  137.6 2.3 %copy.14 = bf16[1,256,2048]{2,1,0:T(8,128)(2,1)} copy(bf16[1,256,2048]{2,1,0:T(8,128)(2,1)} %bitcast.19) | data formatting | bytes 2097152
